TPU v7x, 32 devices: a whole 2x2x4 slice. The times are simulated.
32 devices in a mesh: grp: 4 (over y, core), seq: 2 (over x), head: 4 (over z).
Axes of the slice: x: 2, y: 2, z: 4, core: 2. Of those that a mesh axis runs over, the one named last changes fastest.
Arguments:
- keys: bfloat16 [32, 1024, 1536], P('grp', 'seq', 'head'), may hold values from -6 to 6
- values: bfloat16 [32, 1024, 1536], P('grp', 'seq', 'head'), may hold values from -6 to 6
- log_forget: float32 [32, 24, 1024], P('grp', 'head', 'seq'), may hold values from -0.6 to 0, as said below
- keep: int32 [32, 1024], P('grp', 'seq'), may hold values from 0 to 1, as said below
- merge_weight: float32 [32, 1024], P('grp', 'seq'), may hold values from 0.1 to 10
- lengths: int32 [32], P('grp'), may hold values from 64 to 1024, as said below
- route: int32 [32], P('grp'), may hold values from 0 to 31, as said below
- fresh: bfloat16 [3, 32, 1536], P(None, 'grp', 'head'), may hold values from -7.5 to 7.5
- new_forget: bfloat16 [32, 24], P('grp', 'head'), may hold values from -1 to -0.049804688
- out_weight: bfloat16 [1536, 1536], P('head', 'seq'), may hold values from -0.15625 to 0.15625
Outputs:
- compact_keys: bfloat16 [32, 512, 1536], P('grp', 'seq', 'head')
- compact_values: bfloat16 [32, 512, 1536], P('grp', 'seq', 'head')
- compact_decay: float32 [32, 24, 512], P('grp', 'head', 'seq')
- layer_out: bfloat16 [32, 1536], P('grp', 'seq')
Inputs may be any that keep to these rules, and one draw needn't show every extreme that they name: `keep`: within every aligned block of 64 positions of a request, between 16 and 31 entries are 1, and some block has exactly 31. `lengths`: multiples of 64; the first request of every 8 in order has 1024. `route`: A permutation of the requests. `log_forget`: Negative.
All inputs are finite; a program needn't handle non-finite values.
Results may differ from a plain program's by a relative error of at most 0.0085.
Values may be sent and summed in bfloat16 or wider, within the bound.
No kernel may reach another device: no remote copies, remote signals or barrier semaphores. Data moves between devices by JAX's collectives and lax.ppermute only.
A program may use at most 64 MiB of HBM per device.

v0:
```python
import functools

import jax
import jax.numpy as jnp
from jax import lax
from jax.experimental import pallas as pl
from jax.experimental.pallas import tpu as pltpu
from jax.sharding import PartitionSpec as P

BLOCK = 64
SLOTS = 32
LANES = 128
BLOCK_LOG = BLOCK.bit_length() - 1
SLOT_LOG = SLOTS.bit_length() - 1
EMPTY_LOG = -10000.0
FIRST = 9
SECOND = 4
SIZES = (2, 4, 6, 8, 10, 12, 14)
SURE = 3
EAGER = 5
VMEM_LIMIT = 16 * 1024 * 1024


LIGHT = pl.CostEstimate(flops=1, bytes_accessed=1, transcendentals=0)
MERGE = pl.CostEstimate(flops=1 << 36, bytes_accessed=1, transcendentals=0)


def dot(a, b):
    return lax.dot_general(a, b, (((1,), (0,)), ((), ())), preferred_element_type=jnp.float32)


def dot_nt(a, b):
    return lax.dot_general(a, b, (((1,), (1,)), ((), ())), preferred_element_type=jnp.float32)


def iota(shape, dim):
    return lax.broadcasted_iota(jnp.int32, shape, dim)


def three(x):
    hi = x.astype(jnp.bfloat16).astype(jnp.float32)
    rest = x - hi
    mid = rest.astype(jnp.bfloat16).astype(jnp.float32)
    return hi, mid, rest - mid


def split_dot(x, ones):
    rows = x.shape[0]
    parts = dot(jnp.concatenate(three(x), axis=0).astype(jnp.bfloat16), ones)
    return parts[:rows] + parts[rows : 2 * rows] + parts[2 * rows :]


def half_of(axis, count):
    own = lax.axis_index(axis) if count == 2 else jnp.int32(0)
    return own, 1 - own


def by_row(ref, row):
    picked = jnp.zeros_like(row)
    for r in range(ref.shape[0]):
        picked = jnp.where(row == r, ref[r], picked)
    return picked


def live_blocks(lengths, r, start, most):
    return jnp.clip((lengths[r] - start) >> BLOCK_LOG, 0, most)


def offsets(lengths, start, most):
    total = jnp.int32(0)
    ahead, live = [], []
    for r in range(lengths.shape[0]):
        ahead.append(total)
        live.append(live_blocks(lengths, r, start, most))
        total = total + live[-1]
    return ahead, live, total


def plan(keep, weight, start, len_ref):
    rows, width = keep.shape
    one, two = iota((width, width), 0), iota((width, width), 1)
    same = (one ^ two) < BLOCK
    upto = (same & (one <= two)).astype(jnp.float32).astype(jnp.bfloat16)
    block = same.astype(jnp.float32).astype(jnp.bfloat16)
    kept = keep == 1
    rank = dot(keep.astype(jnp.float32).astype(jnp.bfloat16), upto) - 1.0
    weighted = jnp.where(kept, 0.0, weight)
    share = (weighted / split_dot(weighted, block)).astype(jnp.bfloat16).astype(jnp.float32)
    lane, row = iota((rows, width), 1), iota((rows, width), 0)
    slot = jnp.where(kept, rank.astype(jnp.int32), SLOTS - 1) + (lane >> BLOCK_LOG) * SLOTS
    slot = jnp.where(start + lane < by_row(len_ref, row), slot, -1)
    return slot, jnp.where(kept, 1.0, share)


def select(slot, factor, r):
    width = slot.shape[1]
    shape = (width // 2, width)
    hit = iota(shape, 0) == slot[r : r + 1, :]
    return jnp.where(hit, jnp.broadcast_to(factor[r : r + 1, :], shape), 0.0).astype(jnp.bfloat16)


def lanes(half, width):
    return pl.ds(pl.multiple_of(half * width, width), width)


def far(*arrays):
    return [pltpu.with_memory_space_constraint(x, pltpu.HBM) for x in arrays]


def near(*arrays):
    return [pltpu.with_memory_space_constraint(x, pltpu.VMEM) for x in arrays]


def fetch(pairs, sem):
    copies = [pltpu.make_async_copy(src, dst, sem.at[i]) for i, (src, dst) in enumerate(pairs)]
    for copy in copies:
        copy.start()
    return copies


def first_kernel(n_seq, len_hbm, keep_hbm, weight_hbm, fresh_hbm, gate_hbm, keys, values, *rest):
    out, packed, size_ref, lengths, keep, weight, fresh, gates, raw, row_buf, sem_s, sem_r = rest
    _, sent = half_of("seq", n_seq)
    req, width = keep.shape
    most = width // BLOCK
    small = fetch(
        [
            (len_hbm, lengths),
            (keep_hbm.at[:, lanes(sent, width)], keep),
            (weight_hbm.at[:, lanes(sent, width)], weight),
            (fresh_hbm, fresh),
            (gate_hbm, gates),
        ],
        sem_s,
    )

    def slab(i, r):
        source = (keys, values)[i].at[r, lanes(sent, width), :]
        return pltpu.make_async_copy(source, raw.at[i, r], sem_r.at[i, r])

    eager = min(EAGER, req)
    for r in range(eager):
        for i in range(2):
            slab(i, r).start()
    row_buf[...] = jnp.zeros_like(row_buf)
    for copy in small:
        copy.wait()
    start = lax.axis_index("seq") * (2 * width) + sent * width
    ahead, live, _ = offsets(lengths, start, most)
    needed = [(ahead[r] < FIRST) & (live[r] > 0) for r in range(req)]
    for r in range(eager, req):

        @pl.when(needed[r])
        def _(r=r):
            for i in range(2):
                slab(i, r).start()

    slot, factor = plan(keep[...], weight[...], start, lengths)
    _, _, total = offsets(lengths, width, most)
    choice = jnp.int32(0)
    for size in SIZES:
        choice = choice + (total - FIRST - SECOND > size).astype(jnp.int32)
    size_ref[0] = choice

    new, gate = fresh[...].astype(jnp.float32), gates[...].astype(jnp.float32)
    heads = gate.shape[1]
    lane = iota((req, new.shape[1]), 1)
    size = new.shape[1] // heads
    spread = jnp.zeros((req, new.shape[1]), jnp.float32)
    for h in range(heads):
        inside = (lane >= h * size) & (lane < (h + 1) * size)
        spread = jnp.where(inside, gate[:, h : h + 1], spread)
    packed[...] = jnp.concatenate([new, spread], axis=0).astype(jnp.bfloat16)

    def pack(r):
        chosen = select(slot, factor, r)
        at = pl.ds(pl.multiple_of(ahead[r] * SLOTS, SLOTS), most * SLOTS)
        for i in range(2):
            if r >= eager:
                slab(i, r).wait()
            row_buf[i, at, :] = dot(chosen, raw[i, r]).astype(jnp.bfloat16)

    for r in range(req):
        if r < eager:
            for i in range(2):
                slab(i, r).wait()
        if r < SURE:
            pack(r)
        else:
            pl.when(needed[r])(functools.partial(pack, r))
    out[...] = row_buf[:, : FIRST * SLOTS, :]


def first_part(n_seq, lengths, keep, weight, fresh, gates, keys, values):
    req, pos, width = keys.shape
    half = pos // 2
    hbm = pl.BlockSpec(memory_space=pl.ANY)
    vmem = pl.BlockSpec(memory_space=pltpu.VMEM)
    return pl.pallas_call(
        functools.partial(first_kernel, n_seq),
        out_shape=(
            pltpu.VMEM((2, FIRST * SLOTS, width), jnp.bfloat16),
            pltpu.VMEM((fresh.shape[0] + req, width), jnp.bfloat16),
            jax.ShapeDtypeStruct((1,), jnp.int32),
        ),
        in_specs=[hbm] * 7,
        out_specs=(vmem, vmem, pl.BlockSpec(memory_space=pltpu.SMEM)),
        scratch_shapes=[
            pltpu.SMEM(lengths.shape, jnp.int32),
            pltpu.VMEM((req, half), jnp.int32),
            pltpu.VMEM((req, half), jnp.float32),
            pltpu.VMEM(fresh.shape, fresh.dtype),
            pltpu.VMEM(gates.shape, gates.dtype),
            pltpu.VMEM((2, req, half, width), jnp.bfloat16),
            pltpu.VMEM((2, (FIRST - 1) * SLOTS + half // 2, width), jnp.bfloat16),
            pltpu.SemaphoreType.DMA((5,)),
            pltpu.SemaphoreType.DMA((2, req)),
        ],
        compiler_params=pltpu.CompilerParams(vmem_limit_bytes=VMEM_LIMIT),
        cost_estimate=LIGHT,
        name="compact_first_sent",
    )(*far(lengths, keep, weight, fresh, gates, keys, values))


def own_kernel(
    n_seq, len_ref, keep, weight, gates, keys, values, early, *rest
):
    out_k, out_v, chunk, log_ref, level_ref, total_ref = rest[:6]
    lengths, raw, late, forget, rows, zeros, sem_s, sem_l, sem_r, sem_o, sem_z = rest[6:]
    own, sent = half_of("seq", n_seq)
    seq = lax.axis_index("seq")
    heads, req, pos = gates.shape
    half = pos // 2
    slots = half // 2
    most = half // BLOCK
    first = FIRST // most
    pad = forget.shape[1] // req
    small = fetch([(len_ref, lengths)], sem_s)
    both = ((0, keys), (1, values))
    late_slabs = fetch(
        [
            (source.at[r, lanes(sent, half), :], late.at[i, r - first])
            for r in range(first, req)
            for i, source in both
        ],
        sem_l,
    )
    slabs = fetch(
        [
            (source.at[r, lanes(own, half), :], raw.at[i, r])
            for r in range(req)
            for i, source in both
        ],
        sem_r,
    )
    zeros[...] = jnp.zeros_like(zeros)
    stores = fetch([(zeros, out.at[:, lanes(sent, slots), :]) for out in (out_k, out_v)], sem_z)
    chunk[:, : FIRST * SLOTS, :] = early[...]
    chunk[:, FIRST * SLOTS :, :] = jnp.zeros(
        (2, chunk.shape[1] - FIRST * SLOTS, chunk.shape[2]), chunk.dtype
    )
    for copy in small:
        copy.wait()
    ahead, alive, _ = offsets(lengths, seq * pos + sent * half, most)

    forget[...] = jnp.zeros_like(forget)
    live = seq * pos + iota((req, pos), 1) < by_row(lengths, iota((req, pos), 0))
    for h in range(heads):
        gate = jnp.where(live, gates[h], 0.0)
        for c in range(pos // LANES):
            forget[c, pl.ds(h, req, stride=pad), :] = gate[:, c * LANES : (c + 1) * LANES]
    flat = jnp.concatenate([forget[c] for c in range(pos // LANES)], axis=1)
    total_ref[...] = jnp.broadcast_to(jnp.sum(flat, axis=1, keepdims=True), total_ref.shape)
    one, two = iota((half, half), 0), iota((half, half), 1)
    after = (((one ^ two) < BLOCK) & (one > two)).astype(jnp.float32).astype(jnp.bfloat16)
    ends = iota((pos, slots), 1) >> SLOT_LOG
    begins = iota((pos, slots), 0) >> BLOCK_LOG
    last = iota((req * pad, slots), 1) & (SLOTS - 1) == SLOTS - 1

    for i, h in enumerate((own, sent)):
        slot, factor = plan(
            keep[:, lanes(h, half)], weight[:, lanes(h, half)], seq * pos + h * half, lengths
        )
        near = half // LANES
        inner = split_dot(
            jnp.concatenate([forget[h * near + c] for c in range(near)], axis=1), after
        )
        beyond = split_dot(
            flat, (begins > ends + h * (half // BLOCK)).astype(jnp.float32).astype(jnp.bfloat16)
        )
        spread = jnp.exp(inner)
        high = spread.astype(jnp.bfloat16).astype(jnp.float32)
        planes = three(inner) + (high, spread - high, jnp.ones_like(inner))
        found = []
        for r in range(req):
            chosen = select(slot, factor, r)
            stack = jnp.concatenate([x[r * pad : (r + 1) * pad] for x in planes], axis=0)
            found.append(dot_nt(stack.astype(jnp.bfloat16), chosen))
            if i == 0:
                for k, out in enumerate((out_k, out_v)):
                    slabs[2 * r + k].wait()
                    rows[k, r] = dot(chosen, raw[k, r]).astype(jnp.bfloat16)
                    stores.append(
                        pltpu.make_async_copy(
                            rows.at[k, r], out.at[r, lanes(own, slots), :], sem_o.at[2 * r + k]
                        )
                    )
                    stores[-1].start()
            elif r >= first:
                for k in range(2):
                    late_slabs[2 * (r - first) + k].wait()

                @pl.when((ahead[r] + alive[r] > FIRST) & (alive[r] > 0))
                def _(r=r, chosen=chosen):
                    at = pl.ds(pl.multiple_of(ahead[r] * SLOTS, SLOTS), slots)
                    for k in range(2):
                        chunk[k, at, :] = dot(chosen, late[k, r - first]).astype(jnp.bfloat16)
        at = [
            jnp.concatenate([x[p * pad : (p + 1) * pad] for x in found], axis=0) for p in range(6)
        ]
        filled = at[5] > 0.5
        kept = at[0] + at[1] + at[2]
        merged = jnp.log(jnp.where(filled, at[3] + at[4], 1.0))
        level_ref[i] = jnp.where(filled, jnp.where(last, merged, kept) + beyond, EMPTY_LOG)
        for k in range(heads):
            log_ref[k, :, lanes(h, slots)] = level_ref[i, pl.ds(k, req, stride=pad), :]
    for copy in stores:
        copy.wait()


def own_part(n_seq, lengths, keep, weight, forget, keys, values, early):
    req, pos, width = keys.shape
    heads = forget.shape[0]
    half, slots, pad = pos // 2, pos // 4, -(-heads // 8) * 8
    late = req - FIRST // (half // BLOCK)
    hbm = pl.BlockSpec(memory_space=pl.ANY)
    vmem = pl.BlockSpec(memory_space=pltpu.VMEM)
    whole = pltpu.HBM((req, 2 * slots, width), jnp.bfloat16)
    return pl.pallas_call(
        functools.partial(own_kernel, n_seq),
        out_shape=(
            whole,
            whole,
            pltpu.VMEM((2, req * slots, width), jnp.bfloat16),
            pltpu.VMEM((heads, req, 2 * slots), jnp.float32),
            pltpu.VMEM((2, req * pad, slots), jnp.float32),
            pltpu.VMEM((req * pad, LANES), jnp.float32),
        ),
        in_specs=[vmem] * 4 + [hbm] * 2 + [vmem],
        out_specs=(hbm, hbm, vmem, vmem, vmem, vmem),
        scratch_shapes=[
            pltpu.SMEM(lengths.shape, jnp.int32),
            pltpu.VMEM((2, req, half, width), jnp.bfloat16),
            pltpu.VMEM((2, late, half, width), jnp.bfloat16),
            pltpu.VMEM((pos // LANES, req * pad, LANES), jnp.float32),
            pltpu.VMEM((2, req, slots, width), jnp.bfloat16),
            pltpu.VMEM((req, slots, width), jnp.bfloat16),
            pltpu.SemaphoreType.DMA((1,)),
            pltpu.SemaphoreType.DMA((2 * late,)),
            pltpu.SemaphoreType.DMA((2 * req,)),
            pltpu.SemaphoreType.DMA((2 * req,)),
            pltpu.SemaphoreType.DMA((2,)),
        ],
        compiler_params=pltpu.CompilerParams(vmem_limit_bytes=VMEM_LIMIT),
        cost_estimate=LIGHT,
        name="compact_own",
    )(*near(lengths, keep, weight, forget), *far(keys, values), *near(early))


def attend_kernel(n_seq, n_grp, heads, *refs):
    len_hbm, route_hbm, out_k, out_v, late, level, total = refs[:7]
    tokens, rest = refs[7 : 7 + n_grp], refs[7 + n_grp :]
    _, _, stats_ref, picked_ref, lengths, route, own_rows, scores, sem_s, sem_r = rest
    own, sent = half_of("seq", n_seq)
    kinds, width = picked_ref.shape
    req = kinds // 4
    size = width // heads
    slots = own_rows.shape[2]
    pad = total.shape[0] // req
    small = fetch([(len_hbm, lengths), (route_hbm, route)], sem_s)
    slabs = fetch(
        [
            (out_k.at[:, lanes(own, slots), :], own_rows.at[0]),
            (out_v.at[:, lanes(own, slots), :], own_rows.at[1]),
        ],
        sem_r,
    )
    for copy in small:
        copy.wait()
    start = lax.axis_index("seq") * (4 * slots) + sent * (2 * slots)
    ahead, _, _ = offsets(lengths, start, slots // SLOTS)

    def sent_part(i, r):
        at = pl.multiple_of(ahead[r] * SLOTS, SLOTS)
        return late[i, pl.ds(at, slots), :]

    shape = (kinds, kinds)
    to, frm = iota(shape, 0), iota(shape, 1)
    wanted = by_row(route, to % req)
    me = lax.axis_index("grp")
    picked = jnp.zeros((kinds, width), jnp.float32)
    for k in range(n_grp):
        source = lax.rem(me + n_grp - k, n_grp)
        hit = (to // req == frm // req) & (wanted == source * req + frm % req)
        picked = picked + dot(hit.astype(jnp.float32).astype(jnp.bfloat16), tokens[k][...])
    picked_ref[...] = picked
    for copy in slabs:
        copy.wait()

    lane, row = iota((pad, width), 1), iota((pad, width), 0)
    mine = (lane >= row * size) & (lane < (row + 1) * size)
    for r in range(req):
        query = jnp.where(mine, picked[r : r + 1, :], 0.0).astype(jnp.bfloat16)
        here = slice(r * pad, (r + 1) * pad)
        scores[here, :slots] = dot_nt(query, own_rows[0, r])
        scores[here, slots:] = dot_nt(query, sent_part(0, r))
    logit = scores[...] * (size**-0.5) + jnp.concatenate([level[0], level[1]], axis=1)
    top = jnp.max(logit, axis=1, keepdims=True)
    weights = jnp.exp(logit - top).astype(jnp.bfloat16).astype(jnp.float32)
    mass = jnp.sum(weights, axis=1, keepdims=True)

    def spread_out(column, r):
        return jnp.sum(
            jnp.where(mine, column[r * pad : (r + 1) * pad], 0.0), axis=0, keepdims=True
        )

    for r in range(req):
        w = weights[r * pad : (r + 1) * pad].astype(jnp.bfloat16)
        acc = dot(w[:, :slots], own_rows[1, r]) + dot(w[:, slots:], sent_part(1, r))
        acc = jnp.sum(jnp.where(mine, acc, 0.0), axis=0, keepdims=True)
        for p, x in enumerate((top, mass, total[:, :1])):
            stats_ref[p * req + r : p * req + r + 1, :] = spread_out(x, r)
        stats_ref[3 * req + r : 3 * req + r + 1, :] = acc


def attend_part(n_seq, n_grp, heads, lengths, route, out_k, out_v, late, level, total, tokens):
    req, rows, width = out_k.shape
    slots = rows // 2
    hbm = pl.BlockSpec(memory_space=pl.ANY)
    vmem = pl.BlockSpec(memory_space=pltpu.VMEM)
    whole = pltpu.HBM(out_k.shape, out_k.dtype)
    small = pltpu.VMEM((4 * req, width), jnp.float32)
    return pl.pallas_call(
        functools.partial(attend_kernel, n_seq, n_grp, heads),
        out_shape=(whole, whole, small, small),
        in_specs=[vmem] * 2 + [hbm] * 2 + [vmem] * (3 + n_grp),
        out_specs=(hbm, hbm, vmem, vmem),
        scratch_shapes=[
            pltpu.SMEM(lengths.shape, jnp.int32),
            pltpu.SMEM(route.shape, jnp.int32),
            pltpu.VMEM((2, req, slots, width), jnp.bfloat16),
            pltpu.VMEM((total.shape[0], rows), jnp.float32),
            pltpu.SemaphoreType.DMA((2,)),
            pltpu.SemaphoreType.DMA((2,)),
        ],
        input_output_aliases={2: 0, 3: 1},
        compiler_params=pltpu.CompilerParams(vmem_limit_bytes=VMEM_LIMIT),
        cost_estimate=LIGHT,
        name="attend",
    )(
        *near(lengths, route),
        *far(out_k, out_v),
        *near(late, level, total),
        *near(*tokens),
    )


def merge_kernel(count, relative, size, *refs):
    stats, refs = refs[:count], refs[count:]
    picked_ref, weight_ref, _, later_ref, out_ref = refs
    req, width = later_ref.shape
    seq = lax.axis_index("seq")
    places = [lax.rem(seq + count - k, count) if relative else jnp.int32(k) for k in range(count)]
    tops, masses, totals, accs = [
        [ref[p * req : (p + 1) * req, :] for ref in stats] for p in range(4)
    ]

    def later(place):
        total = jnp.zeros_like(totals[0])
        for k in range(count):
            total = total + jnp.where(places[k] > place, totals[k], 0.0)
        return total

    tops = [tops[k] + later(places[k]) for k in range(count)]
    top = functools.reduce(jnp.maximum, tops)
    scales = [jnp.exp(t - top) for t in tops]
    mass = sum(s * x for s, x in zip(scales, masses))
    acc = sum(s * x for s, x in zip(scales, accs))
    query, key, value, gate = [picked_ref[p * req : (p + 1) * req, :] for p in range(4)]
    one, two = iota((width, width), 0), iota((width, width), 1)
    same = (one // size == two // size).astype(jnp.float32).astype(jnp.bfloat16)
    own = split_dot(query * key, same) * (size**-0.5)
    past = top + gate
    joint = jnp.maximum(past, own)
    scale, self_weight = jnp.exp(past - joint), jnp.exp(own - joint)
    attended = (scale * acc + self_weight * value) / (scale * mass + self_weight)
    later_ref[...] = later(seq)
    out_ref[...] = dot(attended.astype(jnp.bfloat16), weight_ref[...])


def merge_part(stats, relative, picked, out_weight, second, size):
    req, width = stats[0].shape[0] // 4, stats[0].shape[1]
    vmem = pl.BlockSpec(memory_space=pltpu.VMEM)
    return pl.pallas_call(
        functools.partial(merge_kernel, len(stats), relative, size),
        out_shape=(
            pltpu.VMEM((req, width), jnp.float32),
            pltpu.VMEM((req, out_weight.shape[1]), jnp.float32),
        ),
        in_specs=[vmem] * (len(stats) + 2) + [pl.BlockSpec(memory_space=pl.ANY)],
        out_specs=(vmem, vmem),
        compiler_params=pltpu.CompilerParams(vmem_limit_bytes=VMEM_LIMIT),
        cost_estimate=MERGE,
        name="merge_and_project",
    )(*near(*stats, picked, out_weight), second)


def sum_kernel(count, size, *refs):
    parts, (later_ref, log_ref, _, out, decay_ref) = refs[:count], refs[count:]
    me = lax.axis_index("head")
    total = jnp.zeros(out.shape, jnp.float32)
    for place in range(count):
        for k in range(count):
            total = total + jnp.where(lax.rem(me + count - k, count) == place, parts[k][...], 0.0)
    out[...] = total.astype(out.dtype)
    for h in range(log_ref.shape[0]):
        decay_ref[h] = jnp.exp(log_ref[h] + later_ref[:, h * size : h * size + 1])


def sum_part(parts, later, logs, placed, size):
    vmem = pl.BlockSpec(memory_space=pltpu.VMEM)
    return pl.pallas_call(
        functools.partial(sum_kernel, len(parts), size),
        out_shape=(
            pltpu.HBM(parts[0].shape, jnp.bfloat16),
            pltpu.HBM(logs.shape, jnp.float32),
        ),
        in_specs=[vmem] * (len(parts) + 3),
        out_specs=(vmem, vmem),
        compiler_params=pltpu.CompilerParams(vmem_limit_bytes=VMEM_LIMIT),
        cost_estimate=LIGHT,
        name="sum_heads_and_decay",
    )(*parts, later, logs, placed)


def place_kernel(n_seq, first, count, *refs):
    parts, refs = refs[:count], refs[count:]
    len_ref, _, _, out_k, out_v, placed_ref, lengths, sem_s, sem = refs
    _, sent = half_of("seq", n_seq)
    (load,) = fetch([(len_ref, lengths)], sem_s)
    placed_ref[...] = jnp.zeros_like(placed_ref)
    load.wait()
    req, rows, _ = out_k.shape
    slots = rows // 2
    most = slots // SLOTS
    seq = lax.axis_index("seq")
    if n_seq == 2:
        start = (1 - seq) * (4 * slots) + seq * (2 * slots)
    else:
        start = seq * (4 * slots) + sent * (2 * slots)
    ahead, live, _ = offsets(lengths, start, most)
    for phase in ("start", "wait"):
        begin = first
        for p, part in enumerate(parts):
            held = part.shape[1] // SLOTS
            for r in range(req):
                if begin >= (r + 1) * most:
                    continue
                low = jnp.clip(begin - ahead[r], 0, live[r])
                high = jnp.clip(begin + held - ahead[r], 0, live[r])
                for blocks in range(1, min(most, held) + 1):

                    @pl.when(high - low == blocks)
                    def _(p=p, part=part, begin=begin, r=r, low=low, size=blocks * SLOTS):
                        src = pl.multiple_of((ahead[r] + low - begin) * SLOTS, SLOTS)
                        dst = pl.multiple_of(sent * slots + low * SLOTS, SLOTS)
                        for i, out in enumerate((out_k, out_v)):
                            copy = pltpu.make_async_copy(
                                part.at[i, pl.ds(src, size), :],
                                out.at[r, pl.ds(dst, size), :],
                                sem.at[p, i, r],
                            )
                            getattr(copy, phase)()

            begin += held


def place_part(n_seq, first, parts, lengths, out_k, out_v):
    hbm = pl.BlockSpec(memory_space=pl.ANY)
    vmem = pl.BlockSpec(memory_space=pltpu.VMEM)
    shape = pltpu.HBM(out_k.shape, out_k.dtype)
    count = len(parts)
    return pl.pallas_call(
        functools.partial(place_kernel, n_seq, first, count),
        out_shape=(shape, shape, pltpu.VMEM((8, LANES), jnp.float32)),
        in_specs=[vmem] * (count + 1) + [hbm, hbm],
        out_specs=(hbm, hbm, vmem),
        scratch_shapes=[
            pltpu.SMEM(lengths.shape, jnp.int32),
            pltpu.SemaphoreType.DMA((1,)),
            pltpu.SemaphoreType.DMA((count, 2, lengths.shape[0])),
        ],
        input_output_aliases={count + 1: 0, count + 2: 1},
        compiler_params=pltpu.CompilerParams(vmem_limit_bytes=VMEM_LIMIT),
        cost_estimate=LIGHT,
        name="place_received",
    )(*near(*parts, lengths), *far(out_k, out_v))


def others(value, axis):
    count = lax.axis_size(axis)
    return [value] + [
        lax.ppermute(value, axis, [(i, (i + k) % count) for i in range(count)])
        for k in range(1, count)
    ]


def swap(value, n_seq):
    return lax.ppermute(value, "seq", [(0, 1), (1, 0)]) if n_seq == 2 else value


def shards(
    keys, values, log_forget, keep, merge_weight, lengths, route, fresh, new_forget, out_weight
):
    req, pos, width = keys.shape
    heads = log_forget.shape[1]
    size = width // heads
    n_seq, n_grp = lax.axis_size("seq"), lax.axis_size("grp")
    early, packed, choice = first_part(
        n_seq,
        lengths,
        keep,
        merge_weight,
        fresh.reshape(3 * req, width),
        new_forget,
        keys,
        values,
    )
    exchange = functools.partial(swap, n_seq=n_seq)
    first_received = exchange(early)
    tokens = others(packed, "grp")
    out_k, out_v, late, logs, level, total = own_part(
        n_seq,
        lengths,
        keep,
        merge_weight,
        log_forget.transpose(1, 0, 2),
        keys,
        values,
        early,
    )
    begin, end = FIRST * SLOTS, (FIRST + SECOND) * SLOTS
    rest = late.shape[1] - end

    def finish(rows, early, late, logs, level, total, tokens, out_weight, lengths, route, *outs):
        second = exchange(late[:, begin:end])
        out_k, out_v, stats, picked = attend_part(
            n_seq, n_grp, heads, lengths, route, *outs, late, level, total, tokens
        )
        if n_seq == 2:
            all_stats = others(stats, "seq")
        else:
            gathered = lax.all_gather(stats, "seq")
            all_stats = [gathered[i] for i in range(n_seq)]
        third = exchange(late[:, end : end + rows])
        later, partial = merge_part(all_stats, n_seq == 2, picked, out_weight, second, size)
        out_k, out_v, placed = place_part(n_seq, 0, (early, second), lengths, out_k, out_v)
        layer_out, decay = sum_part(others(partial, "head"), later, logs, placed, size)
        out_k, out_v, _ = place_part(n_seq, FIRST + SECOND, (third,), lengths, out_k, out_v)
        return decay, layer_out, out_k, out_v

    operands = (first_received, late, logs, level, total, tokens, out_weight, lengths, route)
    operands += (out_k, out_v)
    if n_seq == 2:
        branches = [
            functools.partial(finish, blocks * SLOTS) for blocks in SIZES + (rest // SLOTS,)
        ]
        decay, layer_out, out_k, out_v = lax.switch(choice[0], branches, *operands)
    else:
        decay, layer_out, out_k, out_v = finish(rest, *operands)
    if n_seq != 2:
        out_k, out_v = (
            lax.all_to_all(x, "seq", split_axis=1, concat_axis=1, tiled=True) for x in (out_k, out_v)
        )
    return out_k, out_v, decay.transpose(1, 0, 2), layer_out


def solution(mesh):
    return jax.shard_map(
        shards,
        mesh=mesh,
        in_specs=(
            P("grp", "seq", "head"),
            P("grp", "seq", "head"),
            P("grp", "head", "seq"),
            P("grp", "seq"),
            P("grp", "seq"),
            P("grp"),
            P("grp"),
            P(None, "grp", "head"),
            P("grp", "head"),
            P("head", "seq"),
        ),
        out_specs=(
            P("grp", "seq", "head"),
            P("grp", "seq", "head"),
            P("grp", "head", "seq"),
            P("grp", "seq"),
        ),
        check_vma=False,
    )
```

profile of v0, /device:TPU:0, one launch (start us, length us, event | category | flops | bytes accessed | tf_op | source)
XLA Modules:
  0.0 37.3 jit_solution(7415802819157103950)
XLA Ops:
  0.6 0.0 copy-start
  0.6 0.0 copy-start.1
  0.7 0.0 copy-start.2
  0.7 0.0 copy-start.3
  0.7 3.2 %compact_first_sent.1 = (bf16[2,288,384]{2,1,0:T(8,128)(2,1)S(1)}, bf16[32,384]{1,0:T(8,128)(2,1)S(1)}, s32[1]{0:T(128)}) custom-call(s32[8]{0:T(128)} %len_ref.1, s32[8,512]{1,0:T(8,128)} %keep.1, f32[8,512]{1,0:T(8,128)} %weight.1, bf16[24,384]{1,0:T(8,128)(2,1)} %bitcast.5, bf16[8,6]{1,0:T(8,128)(2,1)} %gate_hbm.1, bf16[8,512,384]{2,1,0:T(8,128)(2,1)} %keys.3, ...), custom_call_target="tpu_custom_call" | custom-call | flops 1 | bytes 1 | tf_op jit(solution)/shard_map/compact_first_sent/pallas_call | solution.py:199
  3.9 3.4 %collective-permute-start.51 = (bf16[2,288,384]{2,1,0:T(8,128)(2,1)S(1)}, bf16[2,288,384]{2,1,0:T(8,128)(2,1)S(1)}, u32[]{:S(2)}, u32[]{:S(2)}) collective-permute-start(bf16[2,288,384]{2,1,0:T(8,128)(2,1)S(1)} %get-tuple-element.458.early), channel_id=1, source_target_pairs={{0,4},{4,0},{1,5},{5,1},{2,6},{6,2},{3,7},{7,3},{8,12},{12,8},{9,1... | collective-permute-start | bytes 1327112 | tf_op jit(solution)/shard_map/ppermute | solution.py:619
  7.3 0.0 collective-permute-start.48
  7.3 1.9 %collective-permute-start.49 = (bf16[32,384]{1,0:T(8,128)(2,1)S(1)}, bf16[32,384]{1,0:T(8,128)(2,1)S(1)}, u32[]{:S(2)}, u32[]{:S(2)}) collective-permute-start(bf16[32,384]{1,0:T(8,128)(2,1)S(1)} %get-tuple-element.464), channel_id=1, source_target_pairs={{0,16},{8,24},{16,0},{24,8},{1,17},{9,25},{17,1},{25,9},{2,18},{10... | collective-permute-start | bytes 73736 | tf_op jit(solution)/shard_map/ppermute | solution.py:613
  9.2 1.4 %collective-permute-start.50 = (bf16[32,384]{1,0:T(8,128)(2,1)S(1)}, bf16[32,384]{1,0:T(8,128)(2,1)S(1)}, u32[]{:S(2)}, u32[]{:S(2)}) collective-permute-start(bf16[32,384]{1,0:T(8,128)(2,1)S(1)} %get-tuple-element.464), channel_id=1, source_target_pairs={{0,24},{8,0},{16,8},{24,16},{1,25},{9,1},{17,9},{25,17},{2,26},{10... | collective-permute-start | bytes 73736 | tf_op jit(solution)/shard_map/ppermute | solution.py:613
  10.6 0.0 copy-done
  10.6 0.0 copy-done.1
  10.6 0.0 copy-done.2
  10.6 0.0 copy-done.3
  10.6 0.0 copy-start.4
  10.6 0.0 copy-start.5
  10.6 6.7 %compact_own.1 = (bf16[8,256,384]{2,1,0:T(8,128)(2,1)}, bf16[8,256,384]{2,1,0:T(8,128)(2,1)}, bf16[2,1024,384]{2,1,0:T(8,128)(2,1)S(1)}, f32[6,8,256]{2,1,0:T(8,...) custom-call(s32[8]{0:T(128)S(1)} %copy-done, s32[8,512]{1,0:T(8,128)S(1)} %copy-done.2, ...), custom_call_target="tpu_custom_call" | custom-call | flops 1 | bytes 1 | tf_op jit(solution)/shard_map/compact_own/pallas_call | solution.py:339
  18.0 0.0 collective-permute-done.48
  18.0 0.0 collective-permute-done.49
  18.1 0.0 collective-permute-done.50
  18.1 0.0 collective-permute-done.51
  18.1 0.0 copy-done.4
  18.1 0.0 copy-done.5
  18.1 19.0 %conditional.1 = (f32[6,8,256]{2,1,0:T(8,128)}, bf16[8,768]{1,0:T(8,128)(2,1)}, bf16[8,256,384]{2,1,0:T(8,128)(2,1)}, bf16[8,256,384]{2,1,0:T(8,128)(2,1)}) conditional(s32[]{:T(128)} %bitcast.1, (s32[8]{0:T(128)S(1)}, s32[8]{0:T(128)S(1)}, bf16[8,256,384]{2,1,0:T(8,128)(2,1)}, bf16[8,256,384]{2,1,0:T(8,128)(2,1)}, ...), branch_computations={%region_0.0_spmd, %region_1.0_spmd, %region_2.0_spmd, %region_3.0_... | conditional | flops 68719476736 | bytes 7274773 | solution.py:678
  18.3 0.3 collective-permute-start.19
  18.7 2.3 %attend.12 = (bf16[8,256,384]{2,1,0:T(8,128)(2,1)}, bf16[8,256,384]{2,1,0:T(8,128)(2,1)}, f32[32,384]{1,0:T(8,128)S(1)}, f32[32,384]{1,0:T(8,128)S(1)}) custom-call(s32[8]{0:T(128)S(1)} %get-tuple-element.332.refs_0_.refs_2_.refs_1_, s32[8]{0:T(128)S(1)} %get-tuple-element.333.refs_1_, ...), custom_call_target="tpu_custom_call", output_to_operand_aliasing={{0}: (2, {}), {1}: (3, {})} | custom-call | flops 1 | bytes 1 | tf_op jit(solution)/shard_map/cond/branch_4_fun/attend/pallas_call | solution.py:443
  21.0 1.8 %collective-permute-start.18 = (f32[32,384]{1,0:T(8,128)S(1)}, f32[32,384]{1,0:T(8,128)S(1)}, u32[]{:S(2)}, u32[]{:S(2)}) collective-permute-start(f32[32,384]{1,0:T(8,128)S(1)} %get-tuple-element.343.refs_0_), channel_id=1, source_target_pairs={{0,4},{4,0},{1,5},{5,1},{2,6},{6,2},{3,7},{7,3},{8,12},{12,8},{9,1... | collective-permute-start | bytes 147464 | tf_op jit(solution)/shard_map/cond/branch_4_fun/ppermute | solution.py:613
  22.9 0.1 slice.41
  22.9 0.3 collective-permute-start.23
  23.2 3.4 %collective-permute-done.18.refs_1_ = f32[32,384]{1,0:T(8,128)S(1)} collective-permute-done((f32[32,384]{1,0:T(8,128)S(1)}, f32[32,384]{1,0:T(8,128)S(1)}, u32[]{:S(2)}, u32[]{:S(2)}) %collective-permute-start.18) | collective-permute-done | bytes 49184 | tf_op jit(solution)/shard_map/cond/branch_4_fun/ppermute | solution.py:613
  26.6 0.0 collective-permute-done.19.refs_4_.refs_1_
  26.6 0.3 merge_and_project.12
  26.9 1.6 %collective-permute-start.20 = (f32[8,768]{1,0:T(8,128)S(1)}, f32[8,768]{1,0:T(8,128)S(1)}, u32[]{:S(2)}, u32[]{:S(2)}) collective-permute-start(f32[8,768]{1,0:T(8,128)S(1)} %get-tuple-element.346.refs_0_), channel_id=1, source_target_pairs={{0,1},{1,2},{2,3},{3,0},{4,5},{5,6},{6,7},{7,4},{8,9},{9,10},{10,1... | collective-permute-start | bytes 73736 | tf_op jit(solution)/shard_map/cond/branch_4_fun/ppermute | solution.py:613
  28.5 2.6 %collective-permute-start.21 = (f32[8,768]{1,0:T(8,128)S(1)}, f32[8,768]{1,0:T(8,128)S(1)}, u32[]{:S(2)}, u32[]{:S(2)}) collective-permute-start(f32[8,768]{1,0:T(8,128)S(1)} %get-tuple-element.346.refs_0_), channel_id=1, source_target_pairs={{0,2},{1,3},{2,0},{3,1},{4,6},{5,7},{6,4},{7,5},{8,10},{9,11},{10,... | collective-permute-start | bytes 73736 | tf_op jit(solution)/shard_map/cond/branch_4_fun/ppermute | solution.py:613
  31.1 1.3 %collective-permute-start.22 = (f32[8,768]{1,0:T(8,128)S(1)}, f32[8,768]{1,0:T(8,128)S(1)}, u32[]{:S(2)}, u32[]{:S(2)}) collective-permute-start(f32[8,768]{1,0:T(8,128)S(1)} %get-tuple-element.346.refs_0_), channel_id=1, source_target_pairs={{0,3},{1,0},{2,1},{3,2},{4,7},{5,4},{6,5},{7,6},{8,11},{9,8},{10,9... | collective-permute-start | bytes 73736 | tf_op jit(solution)/shard_map/cond/branch_4_fun/ppermute | solution.py:613
  32.5 1.7 %place_received.24 = (bf16[8,256,384]{2,1,0:T(8,128)(2,1)}, bf16[8,256,384]{2,1,0:T(8,128)(2,1)}, f32[8,128]{1,0:T(8,128)S(1)}) custom-call(bf16[2,288,384]{2,1,0:T(8,128)(2,1)S(1)} %get-tuple-element.349.refs_0_, bf16[2,128,384]{2,1,0:T(8,128)(2,1)S(1)} %collective-permute-done.19.refs_4_.refs_1_, ...), custom_call_target="tpu_custom_call", output_to_operand_aliasing={{0}: (3, {}), {1}: (4, {})} | custom-call | flops 1 | bytes 1 | tf_op jit(solution)/shard_map/cond/branch_4_fun/place_received/pallas_call | solution.py:593
  34.1 0.0 collective-permute-done.20.refs_1_
  34.1 0.0 collective-permute-done.21.refs_2_
  34.1 0.8 %collective-permute-done.22.refs_3_ = f32[8,768]{1,0:T(8,128)S(1)} collective-permute-done((f32[8,768]{1,0:T(8,128)S(1)}, f32[8,768]{1,0:T(8,128)S(1)}, u32[]{:S(2)}, u32[]{:S(2)}) %collective-permute-start.22) | collective-permute-done | bytes 24608 | tf_op jit(solution)/shard_map/cond/branch_4_fun/ppermute | solution.py:613
  34.9 0.7 %sum_heads_and_decay.12 = (bf16[8,768]{1,0:T(8,128)(2,1)}, f32[6,8,256]{2,1,0:T(8,128)}) custom-call(f32[8,768]{1,0:T(8,128)S(1)} %get-tuple-element.346.refs_0_, f32[8,768]{1,0:T(8,128)S(1)} %collective-permute-done.20.refs_1_, f32[8,768]{1,0:T(8,128)S(1)} %collective-permute-done.21.refs_2_, f32[8,768]{1,0:T(8,128)S(1)} %collective-permute-done.22.refs_3_, ...), custom_call_target="tpu_custom_call" | custom-call | flops 1 | bytes 1 | tf_op jit(solution)/shard_map/cond/branch_4_fun/sum_heads_and_decay/pallas_call | solution.py:532
  35.7 0.0 collective-permute-done.23.refs_0_
  35.7 1.4 %place_received.25 = (bf16[8,256,384]{2,1,0:T(8,128)(2,1)}, bf16[8,256,384]{2,1,0:T(8,128)(2,1)}, f32[8,128]{1,0:T(8,128)}) custom-call(bf16[2,320,384]{2,1,0:T(8,128)(2,1)S(1)} %collective-permute-done.23.refs_0_, s32[8]{0:T(128)S(1)} %get-tuple-element.332.refs_0_.refs_2_.refs_1_, ...), custom_call_target="tpu_custom_call", output_to_operand_aliasing={{0}: (2, {}), {1}: (3, {})} | custom-call | flops 1 | bytes 1 | tf_op jit(solution)/shard_map/cond/branch_4_fun/place_received/pallas_call | solution.py:593
  (1 shorter events, 0.0 us)
Async XLA Ops:
  0.6 10.0 %copy-start = (s32[8]{0:T(128)S(1)}, s32[8]{0:T(128)}, u32[]{:S(2)}) copy-start(s32[8]{0:T(128)} %len_ref.1) | copy-start | bytes 100
  0.6 10.0 %copy-start.1 = (f32[8,6,512]{2,0,1:T(8,128)S(1)}, f32[8,6,512]{2,0,1:T(8,128)}, u32[]{:S(2)}) copy-start(f32[8,6,512]{2,0,1:T(8,128)} %param.20) | copy-start | bytes 294916
  0.7 10.0 %copy-start.2 = (s32[8,512]{1,0:T(8,128)S(1)}, s32[8,512]{1,0:T(8,128)}, u32[]{:S(2)}) copy-start(s32[8,512]{1,0:T(8,128)} %keep.1) | copy-start | bytes 49156
  0.7 10.0 %copy-start.3 = (f32[8,512]{1,0:T(8,128)S(1)}, f32[8,512]{1,0:T(8,128)}, u32[]{:S(2)}) copy-start(f32[8,512]{1,0:T(8,128)} %weight.1) | copy-start | bytes 49156
  3.9 14.2 %collective-permute-start.51 = (bf16[2,288,384]{2,1,0:T(8,128)(2,1)S(1)}, bf16[2,288,384]{2,1,0:T(8,128)(2,1)S(1)}, u32[]{:S(2)}, u32[]{:S(2)}) collective-permute-start(bf16[2,288,384]{2,1,0:T(8,128)(2,1)S(1)} %get-tuple-element.458.early), channel_id=1, source_target_pairs={{0,4},{4,0},{1,5},{5,1},{2,6},{6,2},{3,7},{7,3},{8,12},{12,8},{9,1... | collective-permute-start | bytes 1327112 | tf_op jit(solution)/shard_map/ppermute | solution.py:619
  7.3 10.8 %collective-permute-start.48 = (bf16[32,384]{1,0:T(8,128)(2,1)S(1)}, bf16[32,384]{1,0:T(8,128)(2,1)S(1)}, u32[]{:S(2)}, u32[]{:S(2)}) collective-permute-start(bf16[32,384]{1,0:T(8,128)(2,1)S(1)} %get-tuple-element.464), channel_id=1, source_target_pairs={{0,8},{8,16},{16,24},{24,0},{1,9},{9,17},{17,25},{25,1},{2,10},{10... | collective-permute-start | bytes 73736 | tf_op jit(solution)/shard_map/ppermute | solution.py:613
  7.3 10.8 %collective-permute-start.49 = (bf16[32,384]{1,0:T(8,128)(2,1)S(1)}, bf16[32,384]{1,0:T(8,128)(2,1)S(1)}, u32[]{:S(2)}, u32[]{:S(2)}) collective-permute-start(bf16[32,384]{1,0:T(8,128)(2,1)S(1)} %get-tuple-element.464), channel_id=1, source_target_pairs={{0,16},{8,24},{16,0},{24,8},{1,17},{9,25},{17,1},{25,9},{2,18},{10... | collective-permute-start | bytes 73736 | tf_op jit(solution)/shard_map/ppermute | solution.py:613
  9.2 8.9 %collective-permute-start.50 = (bf16[32,384]{1,0:T(8,128)(2,1)S(1)}, bf16[32,384]{1,0:T(8,128)(2,1)S(1)}, u32[]{:S(2)}, u32[]{:S(2)}) collective-permute-start(bf16[32,384]{1,0:T(8,128)(2,1)S(1)} %get-tuple-element.464), channel_id=1, source_target_pairs={{0,24},{8,0},{16,8},{24,16},{1,25},{9,1},{17,9},{25,17},{2,26},{10... | collective-permute-start | bytes 73736 | tf_op jit(solution)/shard_map/ppermute | solution.py:613
  10.6 7.5 %copy-start.4 = (s32[8]{0:T(128)S(1)}, s32[8]{0:T(128)}, u32[]{:S(2)}) copy-start(s32[8]{0:T(128)} %param.24) | copy-start | bytes 100
  10.6 7.5 %copy-start.5 = (bf16[384,768]{1,0:T(8,128)(2,1)S(1)}, bf16[384,768]{1,0:T(8,128)(2,1)}, u32[]{:S(2)}) copy-start(bf16[384,768]{1,0:T(8,128)(2,1)} %param.27) | copy-start | bytes 1769476
  18.3 8.3 %collective-permute-start.19 = (bf16[2,128,384]{2,1,0:T(8,128)(2,1)S(1)}, bf16[2,128,384]{2,1,0:T(8,128)(2,1)S(1)}, u32[]{:S(2)}, u32[]{:S(2)}) collective-permute-start(bf16[2,128,384]{2,1,0:T(8,128)(2,1)S(1)} %slice.40), channel_id=1, source_target_pairs={{0,4},{4,0},{1,5},{5,1},{2,6},{6,2},{3,7},{7,3},{8,12},{12,8},{9,1... | collective-permute-start | bytes 589832 | tf_op jit(solution)/shard_map/cond/branch_4_fun/ppermute | solution.py:619
  21.0 5.6 %collective-permute-start.18 = (f32[32,384]{1,0:T(8,128)S(1)}, f32[32,384]{1,0:T(8,128)S(1)}, u32[]{:S(2)}, u32[]{:S(2)}) collective-permute-start(f32[32,384]{1,0:T(8,128)S(1)} %get-tuple-element.343.refs_0_), channel_id=1, source_target_pairs={{0,4},{4,0},{1,5},{5,1},{2,6},{6,2},{3,7},{7,3},{8,12},{12,8},{9,1... | collective-permute-start | bytes 147464 | tf_op jit(solution)/shard_map/cond/branch_4_fun/ppermute | solution.py:613
  22.9 12.7 %collective-permute-start.23 = (bf16[2,320,384]{2,1,0:T(8,128)(2,1)S(1)}, bf16[2,320,384]{2,1,0:T(8,128)(2,1)S(1)}, u32[]{:S(2)}, u32[]{:S(2)}) collective-permute-start(bf16[2,320,384]{2,1,0:T(8,128)(2,1)S(1)} %slice.41), channel_id=1, source_target_pairs={{0,4},{4,0},{1,5},{5,1},{2,6},{6,2},{3,7},{7,3},{8,12},{12,8},{9,1... | collective-permute-start | bytes 1474568 | tf_op jit(solution)/shard_map/cond/branch_4_fun/ppermute | solution.py:619
  26.9 7.2 %collective-permute-start.20 = (f32[8,768]{1,0:T(8,128)S(1)}, f32[8,768]{1,0:T(8,128)S(1)}, u32[]{:S(2)}, u32[]{:S(2)}) collective-permute-start(f32[8,768]{1,0:T(8,128)S(1)} %get-tuple-element.346.refs_0_), channel_id=1, source_target_pairs={{0,1},{1,2},{2,3},{3,0},{4,5},{5,6},{6,7},{7,4},{8,9},{9,10},{10,1... | collective-permute-start | bytes 73736 | tf_op jit(solution)/shard_map/cond/branch_4_fun/ppermute | solution.py:613
  28.5 5.6 %collective-permute-start.21 = (f32[8,768]{1,0:T(8,128)S(1)}, f32[8,768]{1,0:T(8,128)S(1)}, u32[]{:S(2)}, u32[]{:S(2)}) collective-permute-start(f32[8,768]{1,0:T(8,128)S(1)} %get-tuple-element.346.refs_0_), channel_id=1, source_target_pairs={{0,2},{1,3},{2,0},{3,1},{4,6},{5,7},{6,4},{7,5},{8,10},{9,11},{10,... | collective-permute-start | bytes 73736 | tf_op jit(solution)/shard_map/cond/branch_4_fun/ppermute | solution.py:613
  31.1 3.8 %collective-permute-start.22 = (f32[8,768]{1,0:T(8,128)S(1)}, f32[8,768]{1,0:T(8,128)S(1)}, u32[]{:S(2)}, u32[]{:S(2)}) collective-permute-start(f32[8,768]{1,0:T(8,128)S(1)} %get-tuple-element.346.refs_0_), channel_id=1, source_target_pairs={{0,3},{1,0},{2,1},{3,2},{4,7},{5,4},{6,5},{7,6},{8,11},{9,8},{10,9... | collective-permute-start | bytes 73736 | tf_op jit(solution)/shard_map/cond/branch_4_fun/ppermute | solution.py:613
where the time goes:
time: 37.8 us; the launch traced here: 37.3 us
  Pallas kernels  16.4 us (43%)
  starting transfers between devices  14.7 us (39%)
  waiting for transfers between devices  4.2 us (11%)
  between operations  1.56 us (4%)
    ppermute x7, starting transfers between devices, others(): lax.ppermute(value, axis, [(i, (i + k) % count) for i in range(count)])  10.7 us
    pallas_call x1, Pallas kernels, own_part(): pl.pallas_call(functools.partial(own_kernel, n_seq), out_shape=(whole, wh...  6.73 us
    ppermute x7, waiting for transfers between devices, others(): lax.ppermute(value, axis, [(i, (i + k) % count) for i in range(count)])  4.19 us
    ppermute x3, starting transfers between devices, swap(): return lax.ppermute(value, 'seq', [(0, 1), (1, 0)]) if n_seq == 2 else value  4.05 us
    pallas_call x1, Pallas kernels, first_part(): pl.pallas_call(functools.partial(first_kernel, n_seq), out_shape=(pltpu.V...  3.2 us
    pallas_call x2, Pallas kernels, place_part(): pl.pallas_call(functools.partial(place_kernel, n_seq, first, count), out_...  3.08 us
    pallas_call x1, Pallas kernels, attend_part(): pl.pallas_call(functools.partial(attend_kernel, n_seq, n_grp, heads), out...  2.35 us
  transfers between devices with their start and end apart: 10, of which 2 were waited for; matrix products, arithmetic and copies ran while one was open for 0% of the time, Pallas kernels for 32%

commit v1 on v0

--- a/solution.py
+++ b/solution.py
@@ -15,7 +15,7 @@
 EMPTY_LOG = -10000.0
 FIRST = 9
 SECOND = 4
-SIZES = (2, 4, 6, 8, 10, 12, 14)
+SIZES = (4, 7, 9, 11, 12, 13, 15, 17)
 SURE = 3
 EAGER = 5
 VMEM_LIMIT = 16 * 1024 * 1024
@@ -76,12 +76,18 @@
     return ahead, live, total
 
 
-def plan(keep, weight, start, len_ref):
-    rows, width = keep.shape
+def mask(condition):
+    return condition.astype(jnp.float32).astype(jnp.bfloat16)
+
+
+def block_masks(width):
     one, two = iota((width, width), 0), iota((width, width), 1)
     same = (one ^ two) < BLOCK
-    upto = (same & (one <= two)).astype(jnp.float32).astype(jnp.bfloat16)
-    block = same.astype(jnp.float32).astype(jnp.bfloat16)
+    return mask(same & (one <= two)), mask(same), mask(same & (one > two))
+
+
+def plan(keep, weight, start, len_ref, upto, block):
+    rows, width = keep.shape
     kept = keep == 1
     rank = dot(keep.astype(jnp.float32).astype(jnp.bfloat16), upto) - 1.0
     weighted = jnp.where(kept, 0.0, weight)
@@ -143,6 +149,7 @@
         for i in range(2):
             slab(i, r).start()
     row_buf[...] = jnp.zeros_like(row_buf)
+    upto, block, _ = block_masks(width)
     for copy in small:
         copy.wait()
     start = lax.axis_index("seq") * (2 * width) + sent * width
@@ -155,7 +162,7 @@
             for i in range(2):
                 slab(i, r).start()
 
-    slot, factor = plan(keep[...], weight[...], start, lengths)
+    slot, factor = plan(keep[...], weight[...], start, lengths, upto, block)
     _, _, total = offsets(lengths, width, most)
     choice = jnp.int32(0)
     for size in SIZES:
@@ -259,6 +266,7 @@
     chunk[:, FIRST * SLOTS :, :] = jnp.zeros(
         (2, chunk.shape[1] - FIRST * SLOTS, chunk.shape[2]), chunk.dtype
     )
+    upto, block, after = block_masks(half)
     for copy in small:
         copy.wait()
     ahead, alive, _ = offsets(lengths, seq * pos + sent * half, most)
@@ -271,15 +279,18 @@
             forget[c, pl.ds(h, req, stride=pad), :] = gate[:, c * LANES : (c + 1) * LANES]
     flat = jnp.concatenate([forget[c] for c in range(pos // LANES)], axis=1)
     total_ref[...] = jnp.broadcast_to(jnp.sum(flat, axis=1, keepdims=True), total_ref.shape)
-    one, two = iota((half, half), 0), iota((half, half), 1)
-    after = (((one ^ two) < BLOCK) & (one > two)).astype(jnp.float32).astype(jnp.bfloat16)
     ends = iota((pos, slots), 1) >> SLOT_LOG
     begins = iota((pos, slots), 0) >> BLOCK_LOG
     last = iota((req * pad, slots), 1) & (SLOTS - 1) == SLOTS - 1
 
     for i, h in enumerate((own, sent)):
         slot, factor = plan(
-            keep[:, lanes(h, half)], weight[:, lanes(h, half)], seq * pos + h * half, lengths
+            keep[:, lanes(h, half)],
+            weight[:, lanes(h, half)],
+            seq * pos + h * half,
+            lengths,
+            upto,
+            block,
         )
         near = half // LANES
         inner = split_dot(
@@ -568,19 +579,19 @@
                     continue
                 low = jnp.clip(begin - ahead[r], 0, live[r])
                 high = jnp.clip(begin + held - ahead[r], 0, live[r])
-                for blocks in range(1, min(most, held) + 1):
-
-                    @pl.when(high - low == blocks)
-                    def _(p=p, part=part, begin=begin, r=r, low=low, size=blocks * SLOTS):
-                        src = pl.multiple_of((ahead[r] + low - begin) * SLOTS, SLOTS)
-                        dst = pl.multiple_of(sent * slots + low * SLOTS, SLOTS)
-                        for i, out in enumerate((out_k, out_v)):
-                            copy = pltpu.make_async_copy(
-                                part.at[i, pl.ds(src, size), :],
-                                out.at[r, pl.ds(dst, size), :],
-                                sem.at[p, i, r],
-                            )
-                            getattr(copy, phase)()
+                size = pl.multiple_of((high - low) * SLOTS, SLOTS)
+
+                @pl.when(high > low)
+                def _(p=p, part=part, begin=begin, r=r, low=low, size=size):
+                    src = pl.multiple_of((ahead[r] + low - begin) * SLOTS, SLOTS)
+                    dst = pl.multiple_of(sent * slots + low * SLOTS, SLOTS)
+                    for i, out in enumerate((out_k, out_v)):
+                        copy = pltpu.make_async_copy(
+                            part.at[i, pl.ds(src, size), :],
+                            out.at[r, pl.ds(dst, size), :],
+                            sem.at[p, i, r],
+                        )
+                        getattr(copy, phase)()
 
             begin += held
 

time: 37.8 us -> 38.5 us (1.019)
  the two profiles are of different devices: /device:TPU:0 before, /device:TPU:4 now
where the time goes in v1:
time: 38.5 us
  Pallas kernels  17.2 us (45%)
  starting transfers between devices  13.1 us (34%)
  waiting for transfers between devices  6.22 us (16%)
  between operations  1.54 us (4%)
    ppermute x7, starting transfers between devices, others(): lax.ppermute(value, axis, [(i, (i + k) % count) for i in range(count)])  8.05 us
    pallas_call x1, Pallas kernels, own_part(): pl.pallas_call(functools.partial(own_kernel, n_seq), out_shape=(whole, wh...  7.01 us
    ppermute x3, starting transfers between devices, swap(): return lax.ppermute(value, 'seq', [(0, 1), (1, 0)]) if n_seq == 2 else value  5.06 us
    pallas_call x2, Pallas kernels, place_part(): pl.pallas_call(functools.partial(place_kernel, n_seq, first, count), out_...  3.65 us
    ppermute x7, waiting for transfers between devices, others(): lax.ppermute(value, axis, [(i, (i + k) % count) for i in range(count)])  3.55 us
    pallas_call x1, Pallas kernels, first_part(): pl.pallas_call(functools.partial(first_kernel, n_seq), out_shape=(pltpu.V...  3.19 us
    ppermute x3, waiting for transfers between devices, swap(): return lax.ppermute(value, 'seq', [(0, 1), (1, 0)]) if n_seq == 2 else value  2.67 us
    pallas_call x1, Pallas kernels, attend_part(): pl.pallas_call(functools.partial(attend_kernel, n_seq, n_grp, heads), out...  2.35 us
  transfers between devices with their start and end apart: 10, of which 4 were waited for; matrix products, arithmetic and copies ran while one was open for 0% of the time, Pallas kernels for 31%

profile of v1, /device:TPU:4, one launch (start us, length us, event | category | flops | bytes accessed | tf_op | source)
XLA Modules:
  0.0 38.5 jit_solution(14257369468223046854)
XLA Ops:
  0.6 0.0 copy-start
  0.6 0.0 copy-start.1
  0.7 0.0 copy-start.2
  0.7 0.0 copy-start.3
  0.7 3.2 %compact_first_sent.1 = (bf16[2,288,384]{2,1,0:T(8,128)(2,1)S(1)}, bf16[32,384]{1,0:T(8,128)(2,1)S(1)}, s32[1]{0:T(128)}) custom-call(s32[8]{0:T(128)} %len_ref.1, s32[8,512]{1,0:T(8,128)} %keep.1, f32[8,512]{1,0:T(8,128)} %weight.1, bf16[24,384]{1,0:T(8,128)(2,1)} %bitcast.5, bf16[8,6]{1,0:T(8,128)(2,1)} %gate_hbm.1, bf16[8,512,384]{2,1,0:T(8,128)(2,1)} %keys.3, ...), custom_call_target="tpu_custom_call" | custom-call | flops 1 | bytes 1 | tf_op jit(solution)/shard_map/compact_first_sent/pallas_call | solution.py:206
  3.9 1.9 %collective-permute-start.57 = (bf16[2,288,384]{2,1,0:T(8,128)(2,1)S(1)}, bf16[2,288,384]{2,1,0:T(8,128)(2,1)S(1)}, u32[]{:S(2)}, u32[]{:S(2)}) collective-permute-start(bf16[2,288,384]{2,1,0:T(8,128)(2,1)S(1)} %get-tuple-element.513.early), channel_id=1, source_target_pairs={{0,4},{4,0},{1,5},{5,1},{2,6},{6,2},{3,7},{7,3},{8,12},{12,8},{9,1... | collective-permute-start | bytes 1327112 | tf_op jit(solution)/shard_map/ppermute | solution.py:630
  5.8 0.0 collective-permute-start.54
  5.8 0.5 %collective-permute-start.55 = (bf16[32,384]{1,0:T(8,128)(2,1)S(1)}, bf16[32,384]{1,0:T(8,128)(2,1)S(1)}, u32[]{:S(2)}, u32[]{:S(2)}) collective-permute-start(bf16[32,384]{1,0:T(8,128)(2,1)S(1)} %get-tuple-element.519), channel_id=1, source_target_pairs={{0,16},{8,24},{16,0},{24,8},{1,17},{9,25},{17,1},{25,9},{2,18},{10... | collective-permute-start | bytes 73736 | tf_op jit(solution)/shard_map/ppermute | solution.py:624
  6.3 1.4 %collective-permute-start.56 = (bf16[32,384]{1,0:T(8,128)(2,1)S(1)}, bf16[32,384]{1,0:T(8,128)(2,1)S(1)}, u32[]{:S(2)}, u32[]{:S(2)}) collective-permute-start(bf16[32,384]{1,0:T(8,128)(2,1)S(1)} %get-tuple-element.519), channel_id=1, source_target_pairs={{0,24},{8,0},{16,8},{24,16},{1,25},{9,1},{17,9},{25,17},{2,26},{10... | collective-permute-start | bytes 73736 | tf_op jit(solution)/shard_map/ppermute | solution.py:624
  7.7 0.0 copy-done
  7.7 0.0 copy-done.1
  7.7 0.0 copy-done.2
  7.7 0.0 copy-done.3
  7.8 0.0 copy-start.4
  7.8 0.0 copy-start.5
  7.8 7.0 %compact_own.1 = (bf16[8,256,384]{2,1,0:T(8,128)(2,1)}, bf16[8,256,384]{2,1,0:T(8,128)(2,1)}, bf16[2,1024,384]{2,1,0:T(8,128)(2,1)S(1)}, f32[6,8,256]{2,1,0:T(8,...) custom-call(s32[8]{0:T(128)S(1)} %copy-done, s32[8,512]{1,0:T(8,128)S(1)} %copy-done.2, ...), custom_call_target="tpu_custom_call" | custom-call | flops 1 | bytes 1 | tf_op jit(solution)/shard_map/compact_own/pallas_call | solution.py:350
  15.4 0.0 collective-permute-done.54
  15.5 0.0 collective-permute-done.55
  15.5 0.0 collective-permute-done.56
  15.5 0.1 collective-permute-done.57
  15.6 0.0 copy-done.4
  15.6 0.0 copy-done.5
  15.6 22.7 %conditional.1 = (f32[6,8,256]{2,1,0:T(8,128)}, bf16[8,768]{1,0:T(8,128)(2,1)}, bf16[8,256,384]{2,1,0:T(8,128)(2,1)}, bf16[8,256,384]{2,1,0:T(8,128)(2,1)}) conditional(s32[]{:T(128)} %bitcast.1, (s32[8]{0:T(128)S(1)}, s32[8]{0:T(128)S(1)}, bf16[8,256,384]{2,1,0:T(8,128)(2,1)}, bf16[8,256,384]{2,1,0:T(8,128)(2,1)}, ...), branch_computations={%region_0.0_spmd, %region_1.0_spmd, %region_2.0_spmd, %region_3.0_... | conditional | flops 68719476736 | bytes 7274773 | solution.py:689
  15.6 1.6 %collective-permute-start.13 = (bf16[2,128,384]{2,1,0:T(8,128)(2,1)S(1)}, bf16[2,128,384]{2,1,0:T(8,128)(2,1)S(1)}, u32[]{:S(2)}, u32[]{:S(2)}) collective-permute-start(bf16[2,128,384]{2,1,0:T(8,128)(2,1)S(1)} %slice.42), channel_id=1, source_target_pairs={{0,4},{4,0},{1,5},{5,1},{2,6},{6,2},{3,7},{7,3},{8,12},{12,8},{9,1... | collective-permute-start | bytes 589832 | tf_op jit(solution)/shard_map/cond/branch_3_fun/ppermute | solution.py:630
  17.2 2.4 %attend.12 = (bf16[8,256,384]{2,1,0:T(8,128)(2,1)}, bf16[8,256,384]{2,1,0:T(8,128)(2,1)}, f32[32,384]{1,0:T(8,128)S(1)}, f32[32,384]{1,0:T(8,128)S(1)}) custom-call(s32[8]{0:T(128)S(1)} %get-tuple-element.333.refs_0_.refs_2_.refs_1_, s32[8]{0:T(128)S(1)} %get-tuple-element.334.refs_1_, ...), custom_call_target="tpu_custom_call", output_to_operand_aliasing={{0}: (2, {}), {1}: (3, {})} | custom-call | flops 1 | bytes 1 | tf_op jit(solution)/shard_map/cond/branch_3_fun/attend/pallas_call | solution.py:454
  19.6 0.6 %collective-permute-start.12 = (f32[32,384]{1,0:T(8,128)S(1)}, f32[32,384]{1,0:T(8,128)S(1)}, u32[]{:S(2)}, u32[]{:S(2)}) collective-permute-start(f32[32,384]{1,0:T(8,128)S(1)} %get-tuple-element.344.refs_0_), channel_id=1, source_target_pairs={{0,4},{4,0},{1,5},{5,1},{2,6},{6,2},{3,7},{7,3},{8,12},{12,8},{9,1... | collective-permute-start | bytes 147464 | tf_op jit(solution)/shard_map/cond/branch_3_fun/ppermute | solution.py:624
  20.2 0.1 slice.43
  20.2 1.6 %collective-permute-start.17 = (bf16[2,352,384]{2,1,0:T(8,128)(2,1)S(1)}, bf16[2,352,384]{2,1,0:T(8,128)(2,1)S(1)}, u32[]{:S(2)}, u32[]{:S(2)}) collective-permute-start(bf16[2,352,384]{2,1,0:T(8,128)(2,1)S(1)} %slice.43), channel_id=1, source_target_pairs={{0,4},{4,0},{1,5},{5,1},{2,6},{6,2},{3,7},{7,3},{8,12},{12,8},{9,1... | collective-permute-start | bytes 1622024 | tf_op jit(solution)/shard_map/cond/branch_3_fun/ppermute | solution.py:630
  21.8 2.7 %collective-permute-done.12.refs_1_ = f32[32,384]{1,0:T(8,128)S(1)} collective-permute-done((f32[32,384]{1,0:T(8,128)S(1)}, f32[32,384]{1,0:T(8,128)S(1)}, u32[]{:S(2)}, u32[]{:S(2)}) %collective-permute-start.12) | collective-permute-done | bytes 49184 | tf_op jit(solution)/shard_map/cond/branch_3_fun/ppermute | solution.py:624
  24.5 0.0 collective-permute-done.13.refs_4_.refs_1_
  24.5 0.3 merge_and_project.12
  24.9 1.6 %collective-permute-start.14 = (f32[8,768]{1,0:T(8,128)S(1)}, f32[8,768]{1,0:T(8,128)S(1)}, u32[]{:S(2)}, u32[]{:S(2)}) collective-permute-start(f32[8,768]{1,0:T(8,128)S(1)} %get-tuple-element.347.refs_0_), channel_id=1, source_target_pairs={{0,1},{1,2},{2,3},{3,0},{4,5},{5,6},{6,7},{7,4},{8,9},{9,10},{10,1... | collective-permute-start | bytes 73736 | tf_op jit(solution)/shard_map/cond/branch_3_fun/ppermute | solution.py:624
  26.5 2.6 %collective-permute-start.15 = (f32[8,768]{1,0:T(8,128)S(1)}, f32[8,768]{1,0:T(8,128)S(1)}, u32[]{:S(2)}, u32[]{:S(2)}) collective-permute-start(f32[8,768]{1,0:T(8,128)S(1)} %get-tuple-element.347.refs_0_), channel_id=1, source_target_pairs={{0,2},{1,3},{2,0},{3,1},{4,6},{5,7},{6,4},{7,5},{8,10},{9,11},{10,... | collective-permute-start | bytes 73736 | tf_op jit(solution)/shard_map/cond/branch_3_fun/ppermute | solution.py:624
  29.0 1.4 %collective-permute-start.16 = (f32[8,768]{1,0:T(8,128)S(1)}, f32[8,768]{1,0:T(8,128)S(1)}, u32[]{:S(2)}, u32[]{:S(2)}) collective-permute-start(f32[8,768]{1,0:T(8,128)S(1)} %get-tuple-element.347.refs_0_), channel_id=1, source_target_pairs={{0,3},{1,0},{2,1},{3,2},{4,7},{5,4},{6,5},{7,6},{8,11},{9,8},{10,9... | collective-permute-start | bytes 73736 | tf_op jit(solution)/shard_map/cond/branch_3_fun/ppermute | solution.py:624
  30.4 1.7 %place_received.24 = (bf16[8,256,384]{2,1,0:T(8,128)(2,1)}, bf16[8,256,384]{2,1,0:T(8,128)(2,1)}, f32[8,128]{1,0:T(8,128)S(1)}) custom-call(bf16[2,288,384]{2,1,0:T(8,128)(2,1)S(1)} %get-tuple-element.350.refs_0_, bf16[2,128,384]{2,1,0:T(8,128)(2,1)S(1)} %collective-permute-done.13.refs_4_.refs_1_, ...), custom_call_target="tpu_custom_call", output_to_operand_aliasing={{0}: (3, {}), {1}: (4, {})} | custom-call | flops 1 | bytes 1 | tf_op jit(solution)/shard_map/cond/branch_3_fun/place_received/pallas_call | solution.py:604
  32.1 0.0 collective-permute-done.14.refs_1_
  32.1 0.0 collective-permute-done.15.refs_2_
  32.1 0.8 %collective-permute-done.16.refs_3_ = f32[8,768]{1,0:T(8,128)S(1)} collective-permute-done((f32[8,768]{1,0:T(8,128)S(1)}, f32[8,768]{1,0:T(8,128)S(1)}, u32[]{:S(2)}, u32[]{:S(2)}) %collective-permute-start.16) | collective-permute-done | bytes 24608 | tf_op jit(solution)/shard_map/cond/branch_3_fun/ppermute | solution.py:624
  32.9 0.7 %sum_heads_and_decay.12 = (bf16[8,768]{1,0:T(8,128)(2,1)}, f32[6,8,256]{2,1,0:T(8,128)}) custom-call(f32[8,768]{1,0:T(8,128)S(1)} %get-tuple-element.347.refs_0_, f32[8,768]{1,0:T(8,128)S(1)} %collective-permute-done.14.refs_1_, f32[8,768]{1,0:T(8,128)S(1)} %collective-permute-done.15.refs_2_, f32[8,768]{1,0:T(8,128)S(1)} %collective-permute-done.16.refs_3_, ...), custom_call_target="tpu_custom_call" | custom-call | flops 1 | bytes 1 | tf_op jit(solution)/shard_map/cond/branch_3_fun/sum_heads_and_decay/pallas_call | solution.py:543
  33.6 2.5 %collective-permute-done.17.refs_0_ = bf16[2,352,384]{2,1,0:T(8,128)(2,1)S(1)} collective-permute-done((bf16[2,352,384]{2,1,0:T(8,128)(2,1)S(1)}, bf16[2,352,384]{2,1,0:T(8,128)(2,1)S(1)}, u32[]{:S(2)}, u32[]{:S(2)}) %collective-permute-start.17) | collective-permute-done | bytes 540704 | tf_op jit(solution)/shard_map/cond/branch_3_fun/ppermute | solution.py:630
  36.1 2.0 %place_received.25 = (bf16[8,256,384]{2,1,0:T(8,128)(2,1)}, bf16[8,256,384]{2,1,0:T(8,128)(2,1)}, f32[8,128]{1,0:T(8,128)}) custom-call(bf16[2,352,384]{2,1,0:T(8,128)(2,1)S(1)} %collective-permute-done.17.refs_0_, s32[8]{0:T(128)S(1)} %get-tuple-element.333.refs_0_.refs_2_.refs_1_, ...), custom_call_target="tpu_custom_call", output_to_operand_aliasing={{0}: (2, {}), {1}: (3, {})} | custom-call | flops 1 | bytes 1 | tf_op jit(solution)/shard_map/cond/branch_3_fun/place_received/pallas_call | solution.py:604
  (1 shorter events, 0.0 us)
Async XLA Ops:
  0.6 7.1 %copy-start = (s32[8]{0:T(128)S(1)}, s32[8]{0:T(128)}, u32[]{:S(2)}) copy-start(s32[8]{0:T(128)} %len_ref.1) | copy-start | bytes 100
  0.6 7.1 %copy-start.1 = (f32[8,6,512]{2,0,1:T(8,128)S(1)}, f32[8,6,512]{2,0,1:T(8,128)}, u32[]{:S(2)}) copy-start(f32[8,6,512]{2,0,1:T(8,128)} %param.21) | copy-start | bytes 294916
  0.7 7.1 %copy-start.2 = (s32[8,512]{1,0:T(8,128)S(1)}, s32[8,512]{1,0:T(8,128)}, u32[]{:S(2)}) copy-start(s32[8,512]{1,0:T(8,128)} %keep.1) | copy-start | bytes 49156
  0.7 7.1 %copy-start.3 = (f32[8,512]{1,0:T(8,128)S(1)}, f32[8,512]{1,0:T(8,128)}, u32[]{:S(2)}) copy-start(f32[8,512]{1,0:T(8,128)} %weight.1) | copy-start | bytes 49156
  3.9 11.7 %collective-permute-start.57 = (bf16[2,288,384]{2,1,0:T(8,128)(2,1)S(1)}, bf16[2,288,384]{2,1,0:T(8,128)(2,1)S(1)}, u32[]{:S(2)}, u32[]{:S(2)}) collective-permute-start(bf16[2,288,384]{2,1,0:T(8,128)(2,1)S(1)} %get-tuple-element.513.early), channel_id=1, source_target_pairs={{0,4},{4,0},{1,5},{5,1},{2,6},{6,2},{3,7},{7,3},{8,12},{12,8},{9,1... | collective-permute-start | bytes 1327112 | tf_op jit(solution)/shard_map/ppermute | solution.py:630
  5.8 9.6 %collective-permute-start.54 = (bf16[32,384]{1,0:T(8,128)(2,1)S(1)}, bf16[32,384]{1,0:T(8,128)(2,1)S(1)}, u32[]{:S(2)}, u32[]{:S(2)}) collective-permute-start(bf16[32,384]{1,0:T(8,128)(2,1)S(1)} %get-tuple-element.519), channel_id=1, source_target_pairs={{0,8},{8,16},{16,24},{24,0},{1,9},{9,17},{17,25},{25,1},{2,10},{10... | collective-permute-start | bytes 73736 | tf_op jit(solution)/shard_map/ppermute | solution.py:624
  5.8 9.6 %collective-permute-start.55 = (bf16[32,384]{1,0:T(8,128)(2,1)S(1)}, bf16[32,384]{1,0:T(8,128)(2,1)S(1)}, u32[]{:S(2)}, u32[]{:S(2)}) collective-permute-start(bf16[32,384]{1,0:T(8,128)(2,1)S(1)} %get-tuple-element.519), channel_id=1, source_target_pairs={{0,16},{8,24},{16,0},{24,8},{1,17},{9,25},{17,1},{25,9},{2,18},{10... | collective-permute-start | bytes 73736 | tf_op jit(solution)/shard_map/ppermute | solution.py:624
  6.3 9.2 %collective-permute-start.56 = (bf16[32,384]{1,0:T(8,128)(2,1)S(1)}, bf16[32,384]{1,0:T(8,128)(2,1)S(1)}, u32[]{:S(2)}, u32[]{:S(2)}) collective-permute-start(bf16[32,384]{1,0:T(8,128)(2,1)S(1)} %get-tuple-element.519), channel_id=1, source_target_pairs={{0,24},{8,0},{16,8},{24,16},{1,25},{9,1},{17,9},{25,17},{2,26},{10... | collective-permute-start | bytes 73736 | tf_op jit(solution)/shard_map/ppermute | solution.py:624
  7.8 7.9 %copy-start.4 = (s32[8]{0:T(128)S(1)}, s32[8]{0:T(128)}, u32[]{:S(2)}) copy-start(s32[8]{0:T(128)} %param.25) | copy-start | bytes 100
  7.8 7.9 %copy-start.5 = (bf16[384,768]{1,0:T(8,128)(2,1)S(1)}, bf16[384,768]{1,0:T(8,128)(2,1)}, u32[]{:S(2)}) copy-start(bf16[384,768]{1,0:T(8,128)(2,1)} %param.28) | copy-start | bytes 1769476
  15.6 8.9 %collective-permute-start.13 = (bf16[2,128,384]{2,1,0:T(8,128)(2,1)S(1)}, bf16[2,128,384]{2,1,0:T(8,128)(2,1)S(1)}, u32[]{:S(2)}, u32[]{:S(2)}) collective-permute-start(bf16[2,128,384]{2,1,0:T(8,128)(2,1)S(1)} %slice.42), channel_id=1, source_target_pairs={{0,4},{4,0},{1,5},{5,1},{2,6},{6,2},{3,7},{7,3},{8,12},{12,8},{9,1... | collective-permute-start | bytes 589832 | tf_op jit(solution)/shard_map/cond/branch_3_fun/ppermute | solution.py:630
  19.6 5.0 %collective-permute-start.12 = (f32[32,384]{1,0:T(8,128)S(1)}, f32[32,384]{1,0:T(8,128)S(1)}, u32[]{:S(2)}, u32[]{:S(2)}) collective-permute-start(f32[32,384]{1,0:T(8,128)S(1)} %get-tuple-element.344.refs_0_), channel_id=1, source_target_pairs={{0,4},{4,0},{1,5},{5,1},{2,6},{6,2},{3,7},{7,3},{8,12},{12,8},{9,1... | collective-permute-start | bytes 147464 | tf_op jit(solution)/shard_map/cond/branch_3_fun/ppermute | solution.py:624
  20.2 15.9 %collective-permute-start.17 = (bf16[2,352,384]{2,1,0:T(8,128)(2,1)S(1)}, bf16[2,352,384]{2,1,0:T(8,128)(2,1)S(1)}, u32[]{:S(2)}, u32[]{:S(2)}) collective-permute-start(bf16[2,352,384]{2,1,0:T(8,128)(2,1)S(1)} %slice.43), channel_id=1, source_target_pairs={{0,4},{4,0},{1,5},{5,1},{2,6},{6,2},{3,7},{7,3},{8,12},{12,8},{9,1... | collective-permute-start | bytes 1622024 | tf_op jit(solution)/shard_map/cond/branch_3_fun/ppermute | solution.py:630
  24.9 7.2 %collective-permute-start.14 = (f32[8,768]{1,0:T(8,128)S(1)}, f32[8,768]{1,0:T(8,128)S(1)}, u32[]{:S(2)}, u32[]{:S(2)}) collective-permute-start(f32[8,768]{1,0:T(8,128)S(1)} %get-tuple-element.347.refs_0_), channel_id=1, source_target_pairs={{0,1},{1,2},{2,3},{3,0},{4,5},{5,6},{6,7},{7,4},{8,9},{9,10},{10,1... | collective-permute-start | bytes 73736 | tf_op jit(solution)/shard_map/cond/branch_3_fun/ppermute | solution.py:624
  26.5 5.6 %collective-permute-start.15 = (f32[8,768]{1,0:T(8,128)S(1)}, f32[8,768]{1,0:T(8,128)S(1)}, u32[]{:S(2)}, u32[]{:S(2)}) collective-permute-start(f32[8,768]{1,0:T(8,128)S(1)} %get-tuple-element.347.refs_0_), channel_id=1, source_target_pairs={{0,2},{1,3},{2,0},{3,1},{4,6},{5,7},{6,4},{7,5},{8,10},{9,11},{10,... | collective-permute-start | bytes 73736 | tf_op jit(solution)/shard_map/cond/branch_3_fun/ppermute | solution.py:624
  29.0 3.8 %collective-permute-start.16 = (f32[8,768]{1,0:T(8,128)S(1)}, f32[8,768]{1,0:T(8,128)S(1)}, u32[]{:S(2)}, u32[]{:S(2)}) collective-permute-start(f32[8,768]{1,0:T(8,128)S(1)} %get-tuple-element.347.refs_0_), channel_id=1, source_target_pairs={{0,3},{1,0},{2,1},{3,2},{4,7},{5,4},{6,5},{7,6},{8,11},{9,8},{10,9... | collective-permute-start | bytes 73736 | tf_op jit(solution)/shard_map/cond/branch_3_fun/ppermute | solution.py:624

commit v2 on v1

--- a/solution.py
+++ b/solution.py
@@ -13,10 +13,11 @@
 BLOCK_LOG = BLOCK.bit_length() - 1
 SLOT_LOG = SLOTS.bit_length() - 1
 EMPTY_LOG = -10000.0
-FIRST = 9
-SECOND = 4
-SIZES = (4, 7, 9, 11, 12, 13, 15, 17)
-SURE = 3
+FIRST = 8
+SECOND = 3
+SIZES = (6, 9, 11, 13, 14, 15, 17, 19)
+LAST = 4
+SURE = 2
 EAGER = 5
 VMEM_LIMIT = 16 * 1024 * 1024
 
@@ -140,9 +141,12 @@
         sem_s,
     )
 
+    channels = keys.shape[2]
+
     def slab(i, r):
         source = (keys, values)[i].at[r, lanes(sent, width), :]
-        return pltpu.make_async_copy(source, raw.at[i, r], sem_r.at[i, r])
+        target = raw.at[r, :, pl.ds(i * channels, channels)]
+        return pltpu.make_async_copy(source, target, sem_r.at[i, r])
 
     eager = min(EAGER, req)
     for r in range(eager):
@@ -182,10 +186,12 @@
     def pack(r):
         chosen = select(slot, factor, r)
         at = pl.ds(pl.multiple_of(ahead[r] * SLOTS, SLOTS), most * SLOTS)
+        if r >= eager:
+            for i in range(2):
+                slab(i, r).wait()
+        rows = dot(chosen, raw[r]).astype(jnp.bfloat16)
         for i in range(2):
-            if r >= eager:
-                slab(i, r).wait()
-            row_buf[i, at, :] = dot(chosen, raw[i, r]).astype(jnp.bfloat16)
+            row_buf[i, at, :] = rows[:, i * channels : (i + 1) * channels]
 
     for r in range(req):
         if r < eager:
@@ -218,7 +224,7 @@
             pltpu.VMEM((req, half), jnp.float32),
             pltpu.VMEM(fresh.shape, fresh.dtype),
             pltpu.VMEM(gates.shape, gates.dtype),
-            pltpu.VMEM((2, req, half, width), jnp.bfloat16),
+            pltpu.VMEM((req, half, 2 * width), jnp.bfloat16),
             pltpu.VMEM((2, (FIRST - 1) * SLOTS + half // 2, width), jnp.bfloat16),
             pltpu.SemaphoreType.DMA((5,)),
             pltpu.SemaphoreType.DMA((2, req)),
@@ -232,8 +238,8 @@
 def own_kernel(
     n_seq, len_ref, keep, weight, gates, keys, values, early, *rest
 ):
-    out_k, out_v, chunk, log_ref, level_ref, total_ref = rest[:6]
-    lengths, raw, late, forget, rows, zeros, sem_s, sem_l, sem_r, sem_o, sem_z = rest[6:]
+    out_k, out_v, chunk, rows, log_ref, level_ref, total_ref = rest[:7]
+    lengths, raw, late, forget, zeros, sem_s, sem_l, sem_r, sem_o, sem_z = rest[7:]
     own, sent = half_of("seq", n_seq)
     seq = lax.axis_index("seq")
     heads, req, pos = gates.shape
@@ -244,9 +250,14 @@
     pad = forget.shape[1] // req
     small = fetch([(len_ref, lengths)], sem_s)
     both = ((0, keys), (1, values))
+    channels = keys.shape[2]
+
+    def part(i):
+        return pl.ds(i * channels, channels)
+
     late_slabs = fetch(
         [
-            (source.at[r, lanes(sent, half), :], late.at[i, r - first])
+            (source.at[r, lanes(sent, half), :], late.at[r - first, :, part(i)])
             for r in range(first, req)
             for i, source in both
         ],
@@ -254,7 +265,7 @@
     )
     slabs = fetch(
         [
-            (source.at[r, lanes(own, half), :], raw.at[i, r])
+            (source.at[r, lanes(own, half), :], raw.at[r, :, part(i)])
             for r in range(req)
             for i, source in both
         ],
@@ -308,9 +319,11 @@
             stack = jnp.concatenate([x[r * pad : (r + 1) * pad] for x in planes], axis=0)
             found.append(dot_nt(stack.astype(jnp.bfloat16), chosen))
             if i == 0:
+                for k in range(2):
+                    slabs[2 * r + k].wait()
+                made = dot(chosen, raw[r]).astype(jnp.bfloat16)
                 for k, out in enumerate((out_k, out_v)):
-                    slabs[2 * r + k].wait()
-                    rows[k, r] = dot(chosen, raw[k, r]).astype(jnp.bfloat16)
+                    rows[k, r] = made[:, k * channels : (k + 1) * channels]
                     stores.append(
                         pltpu.make_async_copy(
                             rows.at[k, r], out.at[r, lanes(own, slots), :], sem_o.at[2 * r + k]
@@ -324,8 +337,9 @@
                 @pl.when((ahead[r] + alive[r] > FIRST) & (alive[r] > 0))
                 def _(r=r, chosen=chosen):
                     at = pl.ds(pl.multiple_of(ahead[r] * SLOTS, SLOTS), slots)
+                    made = dot(chosen, late[r - first]).astype(jnp.bfloat16)
                     for k in range(2):
-                        chunk[k, at, :] = dot(chosen, late[k, r - first]).astype(jnp.bfloat16)
+                        chunk[k, at, :] = made[:, k * channels : (k + 1) * channels]
         at = [
             jnp.concatenate([x[p * pad : (p + 1) * pad] for x in found], axis=0) for p in range(6)
         ]
@@ -353,18 +367,18 @@
             whole,
             whole,
             pltpu.VMEM((2, req * slots, width), jnp.bfloat16),
+            pltpu.VMEM((2, req, slots, width), jnp.bfloat16),
             pltpu.VMEM((heads, req, 2 * slots), jnp.float32),
             pltpu.VMEM((2, req * pad, slots), jnp.float32),
             pltpu.VMEM((req * pad, LANES), jnp.float32),
         ),
         in_specs=[vmem] * 4 + [hbm] * 2 + [vmem],
-        out_specs=(hbm, hbm, vmem, vmem, vmem, vmem),
+        out_specs=(hbm, hbm, vmem, vmem, vmem, vmem, vmem),
         scratch_shapes=[
             pltpu.SMEM(lengths.shape, jnp.int32),
-            pltpu.VMEM((2, req, half, width), jnp.bfloat16),
-            pltpu.VMEM((2, late, half, width), jnp.bfloat16),
+            pltpu.VMEM((req, half, 2 * width), jnp.bfloat16),
+            pltpu.VMEM((late, half, 2 * width), jnp.bfloat16),
             pltpu.VMEM((pos // LANES, req * pad, LANES), jnp.float32),
-            pltpu.VMEM((2, req, slots, width), jnp.bfloat16),
             pltpu.VMEM((req, slots, width), jnp.bfloat16),
             pltpu.SemaphoreType.DMA((1,)),
             pltpu.SemaphoreType.DMA((2 * late,)),
@@ -379,23 +393,16 @@
 
 
 def attend_kernel(n_seq, n_grp, heads, *refs):
-    len_hbm, route_hbm, out_k, out_v, late, level, total = refs[:7]
-    tokens, rest = refs[7 : 7 + n_grp], refs[7 + n_grp :]
-    _, _, stats_ref, picked_ref, lengths, route, own_rows, scores, sem_s, sem_r = rest
-    own, sent = half_of("seq", n_seq)
+    len_hbm, route_hbm, own_rows, late, level, total = refs[:6]
+    tokens, rest = refs[6 : 6 + n_grp], refs[6 + n_grp :]
+    stats_ref, picked_ref, lengths, route, scores, sem_s = rest
+    _, sent = half_of("seq", n_seq)
     kinds, width = picked_ref.shape
     req = kinds // 4
     size = width // heads
     slots = own_rows.shape[2]
     pad = total.shape[0] // req
     small = fetch([(len_hbm, lengths), (route_hbm, route)], sem_s)
-    slabs = fetch(
-        [
-            (out_k.at[:, lanes(own, slots), :], own_rows.at[0]),
-            (out_v.at[:, lanes(own, slots), :], own_rows.at[1]),
-        ],
-        sem_r,
-    )
     for copy in small:
         copy.wait()
     start = lax.axis_index("seq") * (4 * slots) + sent * (2 * slots)
@@ -415,8 +422,6 @@
         hit = (to // req == frm // req) & (wanted == source * req + frm % req)
         picked = picked + dot(hit.astype(jnp.float32).astype(jnp.bfloat16), tokens[k][...])
     picked_ref[...] = picked
-    for copy in slabs:
-        copy.wait()
 
     lane, row = iota((pad, width), 1), iota((pad, width), 0)
     mine = (lane >= row * size) & (lane < (row + 1) * size)
@@ -444,36 +449,25 @@
         stats_ref[3 * req + r : 3 * req + r + 1, :] = acc
 
 
-def attend_part(n_seq, n_grp, heads, lengths, route, out_k, out_v, late, level, total, tokens):
-    req, rows, width = out_k.shape
-    slots = rows // 2
-    hbm = pl.BlockSpec(memory_space=pl.ANY)
+def attend_part(n_seq, n_grp, heads, lengths, route, own_rows, late, level, total, tokens):
+    _, req, slots, width = own_rows.shape
     vmem = pl.BlockSpec(memory_space=pltpu.VMEM)
-    whole = pltpu.HBM(out_k.shape, out_k.dtype)
     small = pltpu.VMEM((4 * req, width), jnp.float32)
     return pl.pallas_call(
         functools.partial(attend_kernel, n_seq, n_grp, heads),
-        out_shape=(whole, whole, small, small),
-        in_specs=[vmem] * 2 + [hbm] * 2 + [vmem] * (3 + n_grp),
-        out_specs=(hbm, hbm, vmem, vmem),
+        out_shape=(small, small),
+        in_specs=[vmem] * (6 + n_grp),
+        out_specs=(vmem, vmem),
         scratch_shapes=[
             pltpu.SMEM(lengths.shape, jnp.int32),
             pltpu.SMEM(route.shape, jnp.int32),
-            pltpu.VMEM((2, req, slots, width), jnp.bfloat16),
-            pltpu.VMEM((total.shape[0], rows), jnp.float32),
-            pltpu.SemaphoreType.DMA((2,)),
+            pltpu.VMEM((total.shape[0], 2 * slots), jnp.float32),
             pltpu.SemaphoreType.DMA((2,)),
         ],
-        input_output_aliases={2: 0, 3: 1},
         compiler_params=pltpu.CompilerParams(vmem_limit_bytes=VMEM_LIMIT),
         cost_estimate=LIGHT,
         name="attend",
-    )(
-        *near(lengths, route),
-        *far(out_k, out_v),
-        *near(late, level, total),
-        *near(*tokens),
-    )
+    )(*near(lengths, route, own_rows, late, level, total), *near(*tokens))
 
 
 def merge_kernel(count, relative, size, *refs):
@@ -650,7 +644,7 @@
     exchange = functools.partial(swap, n_seq=n_seq)
     first_received = exchange(early)
     tokens = others(packed, "grp")
-    out_k, out_v, late, logs, level, total = own_part(
+    out_k, out_v, late, own_rows, logs, level, total = own_part(
         n_seq,
         lengths,
         keep,
@@ -663,25 +657,30 @@
     begin, end = FIRST * SLOTS, (FIRST + SECOND) * SLOTS
     rest = late.shape[1] - end
 
-    def finish(rows, early, late, logs, level, total, tokens, out_weight, lengths, route, *outs):
+    def finish(rows, early, late, own_rows, logs, level, total, tokens, *others_in):
+        out_weight, lengths, route, out_k, out_v = others_in
         second = exchange(late[:, begin:end])
-        out_k, out_v, stats, picked = attend_part(
-            n_seq, n_grp, heads, lengths, route, *outs, late, level, total, tokens
+        stats, picked = attend_part(
+            n_seq, n_grp, heads, lengths, route, own_rows, late, level, total, tokens
         )
         if n_seq == 2:
             all_stats = others(stats, "seq")
         else:
             gathered = lax.all_gather(stats, "seq")
             all_stats = [gathered[i] for i in range(n_seq)]
-        third = exchange(late[:, end : end + rows])
+        ends = [end, end + rows]
+        if rows > 2 * LAST * SLOTS:
+            ends.insert(1, end + rows - LAST * SLOTS)
+        third = [exchange(late[:, low:high]) for low, high in zip(ends, ends[1:])]
         later, partial = merge_part(all_stats, n_seq == 2, picked, out_weight, second, size)
         out_k, out_v, placed = place_part(n_seq, 0, (early, second), lengths, out_k, out_v)
         layer_out, decay = sum_part(others(partial, "head"), later, logs, placed, size)
-        out_k, out_v, _ = place_part(n_seq, FIRST + SECOND, (third,), lengths, out_k, out_v)
+        for low, part in zip(ends, third):
+            out_k, out_v, _ = place_part(n_seq, low // SLOTS, (part,), lengths, out_k, out_v)
         return decay, layer_out, out_k, out_v
 
-    operands = (first_received, late, logs, level, total, tokens, out_weight, lengths, route)
-    operands += (out_k, out_v)
+    operands = (first_received, late, own_rows, logs, level, total, tokens)
+    operands += (out_weight, lengths, route, out_k, out_v)
     if n_seq == 2:
         branches = [
             functools.partial(finish, blocks * SLOTS) for blocks in SIZES + (rest // SLOTS,)

time: 38.5 us -> 38.2 us (level)
  the two profiles are of different devices: /device:TPU:4 before, /device:TPU:0 now
where the time goes in v2:
time: 38.2 us; the launch traced here: 38.5 us
  Pallas kernels  16.5 us (43%)
  starting transfers between devices  15.6 us (41%)
  waiting for transfers between devices  4.42 us (12%)
  between operations  1.56 us (4%)
    ppermute x7, starting transfers between devices, others(): lax.ppermute(value, axis, [(i, (i + k) % count) for i in range(count)])  9.88 us
    pallas_call x1, Pallas kernels, own_part(): pl.pallas_call(functools.partial(own_kernel, n_seq), out_shape=(whole, wh...  6.09 us
    ppermute x4, starting transfers between devices, swap(): return lax.ppermute(value, 'seq', [(0, 1), (1, 0)]) if n_seq == 2 else value  5.74 us
    pallas_call x3, Pallas kernels, place_part(): pl.pallas_call(functools.partial(place_kernel, n_seq, first, count), out_...  4.98 us
    ppermute x7, waiting for transfers between devices, others(): lax.ppermute(value, axis, [(i, (i + k) % count) for i in range(count)])  4.41 us
    pallas_call x1, Pallas kernels, first_part(): pl.pallas_call(functools.partial(first_kernel, n_seq), out_shape=(pltpu.V...  2.72 us
    pallas_call x1, Pallas kernels, attend_part(): pl.pallas_call(functools.partial(attend_kernel, n_seq, n_grp, heads), out...  1.64 us
  transfers between devices with their start and end apart: 11, of which 2 were waited for; matrix products, arithmetic and copies ran while one was open for 0% of the time, Pallas kernels for 32%

profile of v2, /device:TPU:0, one launch (start us, length us, event | category | flops | bytes accessed | tf_op | source)
XLA Modules:
  0.0 38.5 jit_solution(500913547572000482)
XLA Ops:
  0.6 0.0 copy-start
  0.6 0.0 copy-start.1
  0.7 0.0 copy-start.2
  0.7 0.0 copy-start.3
  0.7 2.7 %compact_first_sent.1 = (bf16[2,256,384]{2,1,0:T(8,128)(2,1)S(1)}, bf16[32,384]{1,0:T(8,128)(2,1)S(1)}, s32[1]{0:T(128)}) custom-call(s32[8]{0:T(128)} %len_ref.1, s32[8,512]{1,0:T(8,128)} %keep.1, f32[8,512]{1,0:T(8,128)} %weight.1, bf16[24,384]{1,0:T(8,128)(2,1)} %bitcast.5, bf16[8,6]{1,0:T(8,128)(2,1)} %gate_hbm.1, bf16[8,512,384]{2,1,0:T(8,128)(2,1)} %keys.3, ...), custom_call_target="tpu_custom_call" | custom-call | flops 1 | bytes 1 | tf_op jit(solution)/shard_map/compact_first_sent/pallas_call | solution.py:212
  3.4 3.0 %collective-permute-start.65 = (bf16[2,256,384]{2,1,0:T(8,128)(2,1)S(1)}, bf16[2,256,384]{2,1,0:T(8,128)(2,1)S(1)}, u32[]{:S(2)}, u32[]{:S(2)}) collective-permute-start(bf16[2,256,384]{2,1,0:T(8,128)(2,1)S(1)} %get-tuple-element.539.early), channel_id=1, source_target_pairs={{0,4},{4,0},{1,5},{5,1},{2,6},{6,2},{3,7},{7,3},{8,12},{12,8},{9,1... | collective-permute-start | bytes 1179656 | tf_op jit(solution)/shard_map/ppermute | solution.py:624
  6.4 0.0 collective-permute-start.62
  6.4 2.2 %collective-permute-start.63 = (bf16[32,384]{1,0:T(8,128)(2,1)S(1)}, bf16[32,384]{1,0:T(8,128)(2,1)S(1)}, u32[]{:S(2)}, u32[]{:S(2)}) collective-permute-start(bf16[32,384]{1,0:T(8,128)(2,1)S(1)} %get-tuple-element.544), channel_id=1, source_target_pairs={{0,16},{8,24},{16,0},{24,8},{1,17},{9,25},{17,1},{25,9},{2,18},{10... | collective-permute-start | bytes 73736 | tf_op jit(solution)/shard_map/ppermute | solution.py:618
  8.7 1.4 %collective-permute-start.64 = (bf16[32,384]{1,0:T(8,128)(2,1)S(1)}, bf16[32,384]{1,0:T(8,128)(2,1)S(1)}, u32[]{:S(2)}, u32[]{:S(2)}) collective-permute-start(bf16[32,384]{1,0:T(8,128)(2,1)S(1)} %get-tuple-element.544), channel_id=1, source_target_pairs={{0,24},{8,0},{16,8},{24,16},{1,25},{9,1},{17,9},{25,17},{2,26},{10... | collective-permute-start | bytes 73736 | tf_op jit(solution)/shard_map/ppermute | solution.py:618
  10.1 0.0 copy-done
  10.1 0.0 copy-done.1
  10.1 0.0 copy-done.2
  10.1 0.0 copy-done.3
  10.1 0.0 copy-start.4
  10.1 0.0 copy-start.5
  10.1 6.1 %compact_own.1 = (bf16[8,256,384]{2,1,0:T(8,128)(2,1)}, bf16[8,256,384]{2,1,0:T(8,128)(2,1)}, bf16[2,1024,384]{2,1,0:T(8,128)(2,1)S(1)}, bf16[2,8,128,384]{3,2,1...) custom-call(s32[8]{0:T(128)S(1)} %copy-done, ...), custom_call_target="tpu_custom_call" | custom-call | flops 1 | bytes 1 | tf_op jit(solution)/shard_map/compact_own/pallas_call | solution.py:364
  16.9 0.0 collective-permute-done.62
  16.9 0.0 collective-permute-done.63
  16.9 0.0 collective-permute-done.64
  16.9 0.0 collective-permute-done.65
  16.9 0.0 copy-done.4
  16.9 0.0 copy-done.5
  16.9 21.4 %conditional.1 = (f32[6,8,256]{2,1,0:T(8,128)}, bf16[8,768]{1,0:T(8,128)(2,1)}, bf16[8,256,384]{2,1,0:T(8,128)(2,1)}, bf16[8,256,384]{2,1,0:T(8,128)(2,1)}) conditional(s32[]{:T(128)} %bitcast.1, (s32[8]{0:T(128)S(1)}, s32[8]{0:T(128)S(1)}, bf16[2,8,128,384]{3,2,1,0:T(8,128)(2,1)S(1)}, ...), branch_computations={%region_0.0_spmd, %region_1.0_spmd, %region_2.0_spmd, %region_3.0_... | conditional | flops 68719476736 | bytes 7569726 | solution.py:688
  17.0 0.6 %collective-permute-start.7 = (bf16[2,96,384]{2,1,0:T(8,128)(2,1)S(1)}, bf16[2,96,384]{2,1,0:T(8,128)(2,1)S(1)}, u32[]{:S(2)}, u32[]{:S(2)}) collective-permute-start(bf16[2,96,384]{2,1,0:T(8,128)(2,1)S(1)} %slice.54), channel_id=1, source_target_pairs={{0,4},{4,0},{1,5},{5,1},{2,6},{6,2},{3,7},{7,3},{8,12},{12,8},{9,1... | collective-permute-start | bytes 442376 | tf_op jit(solution)/shard_map/cond/branch_1_fun/ppermute | solution.py:624
  17.6 1.6 %attend.10 = (f32[32,384]{1,0:T(8,128)S(1)}, f32[32,384]{1,0:T(8,128)S(1)}) custom-call(s32[8]{0:T(128)S(1)} %get-tuple-element.296.refs_0_.refs_2_.refs_1_, s32[8]{0:T(128)S(1)} %get-tuple-element.297.refs_1_, bf16[2,8,128,384]{3,2,1,0:T(8,128)(2,1)S(1)} %get-tuple-element.298.refs_2_, bf16[2,1024,384]{2,1,0:T(8,128)(2,1)S(1)} %get-tuple-element.299.refs_3_, ...), custom_call_target="tpu_custom_call" | custom-call | flops 1 | bytes 1 | tf_op jit(solution)/shard_map/cond/branch_1_fun/attend/pallas_call | solution.py:456
  19.2 1.6 %collective-permute-start.6 = (f32[32,384]{1,0:T(8,128)S(1)}, f32[32,384]{1,0:T(8,128)S(1)}, u32[]{:S(2)}, u32[]{:S(2)}) collective-permute-start(f32[32,384]{1,0:T(8,128)S(1)} %get-tuple-element.306.refs_0_), channel_id=1, source_target_pairs={{0,4},{4,0},{1,5},{5,1},{2,6},{6,2},{3,7},{7,3},{8,12},{12,8},{9,1... | collective-permute-start | bytes 147464 | tf_op jit(solution)/shard_map/cond/branch_1_fun/ppermute | solution.py:618
  20.8 0.6 %collective-permute-start.12 = (bf16[2,160,384]{2,1,0:T(8,128)(2,1)S(1)}, bf16[2,160,384]{2,1,0:T(8,128)(2,1)S(1)}, u32[]{:S(2)}, u32[]{:S(2)}) collective-permute-start(bf16[2,160,384]{2,1,0:T(8,128)(2,1)S(1)} %slice.56), channel_id=1, source_target_pairs={{0,4},{4,0},{1,5},{5,1},{2,6},{6,2},{3,7},{7,3},{8,12},{12,8},{9,1... | collective-permute-start | bytes 737288 | tf_op jit(solution)/shard_map/cond/branch_1_fun/ppermute | solution.py:624
  21.4 1.6 %collective-permute-start.11 = (bf16[2,128,384]{2,1,0:T(8,128)(2,1)S(1)}, bf16[2,128,384]{2,1,0:T(8,128)(2,1)S(1)}, u32[]{:S(2)}, u32[]{:S(2)}) collective-permute-start(bf16[2,128,384]{2,1,0:T(8,128)(2,1)S(1)} %slice.55), channel_id=1, source_target_pairs={{0,4},{4,0},{1,5},{5,1},{2,6},{6,2},{3,7},{7,3},{8,12},{12,8},{9,1... | collective-permute-start | bytes 589832 | tf_op jit(solution)/shard_map/cond/branch_1_fun/ppermute | solution.py:624
  23.0 1.4 %collective-permute-done.6.refs_1_ = f32[32,384]{1,0:T(8,128)S(1)} collective-permute-done((f32[32,384]{1,0:T(8,128)S(1)}, f32[32,384]{1,0:T(8,128)S(1)}, u32[]{:S(2)}, u32[]{:S(2)}) %collective-permute-start.6) | collective-permute-done | bytes 49184 | tf_op jit(solution)/shard_map/cond/branch_1_fun/ppermute | solution.py:618
  24.4 0.0 collective-permute-done.7.refs_4_.refs_1_
  24.4 0.3 merge_and_project.10
  24.8 3.6 %collective-permute-start.10 = (f32[8,768]{1,0:T(8,128)S(1)}, f32[8,768]{1,0:T(8,128)S(1)}, u32[]{:S(2)}, u32[]{:S(2)}) collective-permute-start(f32[8,768]{1,0:T(8,128)S(1)} %get-tuple-element.309.refs_0_), channel_id=1, source_target_pairs={{0,3},{1,0},{2,1},{3,2},{4,7},{5,4},{6,5},{7,6},{8,11},{9,8},{10,9... | collective-permute-start | bytes 73736 | tf_op jit(solution)/shard_map/cond/branch_1_fun/ppermute | solution.py:618
  28.4 0.0 collective-permute-start.8
  28.4 1.0 %collective-permute-start.9 = (f32[8,768]{1,0:T(8,128)S(1)}, f32[8,768]{1,0:T(8,128)S(1)}, u32[]{:S(2)}, u32[]{:S(2)}) collective-permute-start(f32[8,768]{1,0:T(8,128)S(1)} %get-tuple-element.309.refs_0_), channel_id=1, source_target_pairs={{0,2},{1,3},{2,0},{3,1},{4,6},{5,7},{6,4},{7,5},{8,10},{9,11},{10,... | collective-permute-start | bytes 73736 | tf_op jit(solution)/shard_map/cond/branch_1_fun/ppermute | solution.py:618
  29.4 1.6 %place_received.28 = (bf16[8,256,384]{2,1,0:T(8,128)(2,1)}, bf16[8,256,384]{2,1,0:T(8,128)(2,1)}, f32[8,128]{1,0:T(8,128)S(1)}) custom-call(bf16[2,256,384]{2,1,0:T(8,128)(2,1)S(1)} %get-tuple-element.312.refs_0_, bf16[2,96,384]{2,1,0:T(8,128)(2,1)S(1)} %collective-permute-done.7.refs_4_.refs_1_, ...), custom_call_target="tpu_custom_call", output_to_operand_aliasing={{0}: (3, {}), {1}: (4, {})} | custom-call | flops 1 | bytes 1 | tf_op jit(solution)/shard_map/cond/branch_1_fun/place_received/pallas_call | solution.py:598
  31.0 0.0 collective-permute-done.10.refs_3_
  31.0 3.0 %collective-permute-done.8.refs_1_ = f32[8,768]{1,0:T(8,128)S(1)} collective-permute-done((f32[8,768]{1,0:T(8,128)S(1)}, f32[8,768]{1,0:T(8,128)S(1)}, u32[]{:S(2)}, u32[]{:S(2)}) %collective-permute-start.8) | collective-permute-done | bytes 24608 | tf_op jit(solution)/shard_map/cond/branch_1_fun/ppermute | solution.py:618
  34.0 0.0 collective-permute-done.9.refs_2_
  34.0 0.7 %sum_heads_and_decay.10 = (bf16[8,768]{1,0:T(8,128)(2,1)}, f32[6,8,256]{2,1,0:T(8,128)}) custom-call(f32[8,768]{1,0:T(8,128)S(1)} %get-tuple-element.309.refs_0_, f32[8,768]{1,0:T(8,128)S(1)} %collective-permute-done.8.refs_1_, f32[8,768]{1,0:T(8,128)S(1)} %collective-permute-done.9.refs_2_, f32[8,768]{1,0:T(8,128)S(1)} %collective-permute-done.10.refs_3_, ...), custom_call_target="tpu_custom_call" | custom-call | flops 1 | bytes 1 | tf_op jit(solution)/shard_map/cond/branch_1_fun/sum_heads_and_decay/pallas_call | solution.py:537
  34.7 0.0 collective-permute-done.12.refs_0_
  34.7 2.0 %place_received.29 = (bf16[8,256,384]{2,1,0:T(8,128)(2,1)}, bf16[8,256,384]{2,1,0:T(8,128)(2,1)}, f32[8,128]{1,0:T(8,128)}) custom-call(bf16[2,160,384]{2,1,0:T(8,128)(2,1)S(1)} %collective-permute-done.12.refs_0_, s32[8]{0:T(128)S(1)} %get-tuple-element.296.refs_0_.refs_2_.refs_1_, ...), custom_call_target="tpu_custom_call", output_to_operand_aliasing={{0}: (2, {}), {1}: (3, {})} | custom-call | flops 1 | bytes 1 | tf_op jit(solution)/shard_map/cond/branch_1_fun/place_received/pallas_call | solution.py:598
  36.7 0.0 collective-permute-done.11.refs_0_
  36.7 1.4 %place_received.30 = (bf16[8,256,384]{2,1,0:T(8,128)(2,1)}, bf16[8,256,384]{2,1,0:T(8,128)(2,1)}, f32[8,128]{1,0:T(8,128)}) custom-call(bf16[2,128,384]{2,1,0:T(8,128)(2,1)S(1)} %collective-permute-done.11.refs_0_, s32[8]{0:T(128)S(1)} %get-tuple-element.296.refs_0_.refs_2_.refs_1_, ...), custom_call_target="tpu_custom_call", output_to_operand_aliasing={{0}: (2, {}), {1}: (3, {})} | custom-call | flops 1 | bytes 1 | tf_op jit(solution)/shard_map/cond/branch_1_fun/place_received/pallas_call | solution.py:598
  (3 shorter events, 0.1 us)
Async XLA Ops:
  0.6 9.5 %copy-start = (s32[8]{0:T(128)S(1)}, s32[8]{0:T(128)}, u32[]{:S(2)}) copy-start(s32[8]{0:T(128)} %len_ref.1) | copy-start | bytes 100
  0.6 9.4 %copy-start.1 = (f32[8,6,512]{2,0,1:T(8,128)S(1)}, f32[8,6,512]{2,0,1:T(8,128)}, u32[]{:S(2)}) copy-start(f32[8,6,512]{2,0,1:T(8,128)} %param.21) | copy-start | bytes 294916
  0.7 9.4 %copy-start.2 = (s32[8,512]{1,0:T(8,128)S(1)}, s32[8,512]{1,0:T(8,128)}, u32[]{:S(2)}) copy-start(s32[8,512]{1,0:T(8,128)} %keep.1) | copy-start | bytes 49156
  0.7 9.4 %copy-start.3 = (f32[8,512]{1,0:T(8,128)S(1)}, f32[8,512]{1,0:T(8,128)}, u32[]{:S(2)}) copy-start(f32[8,512]{1,0:T(8,128)} %weight.1) | copy-start | bytes 49156
  3.4 13.5 %collective-permute-start.65 = (bf16[2,256,384]{2,1,0:T(8,128)(2,1)S(1)}, bf16[2,256,384]{2,1,0:T(8,128)(2,1)S(1)}, u32[]{:S(2)}, u32[]{:S(2)}) collective-permute-start(bf16[2,256,384]{2,1,0:T(8,128)(2,1)S(1)} %get-tuple-element.539.early), channel_id=1, source_target_pairs={{0,4},{4,0},{1,5},{5,1},{2,6},{6,2},{3,7},{7,3},{8,12},{12,8},{9,1... | collective-permute-start | bytes 1179656 | tf_op jit(solution)/shard_map/ppermute | solution.py:624
  6.4 10.5 %collective-permute-start.62 = (bf16[32,384]{1,0:T(8,128)(2,1)S(1)}, bf16[32,384]{1,0:T(8,128)(2,1)S(1)}, u32[]{:S(2)}, u32[]{:S(2)}) collective-permute-start(bf16[32,384]{1,0:T(8,128)(2,1)S(1)} %get-tuple-element.544), channel_id=1, source_target_pairs={{0,8},{8,16},{16,24},{24,0},{1,9},{9,17},{17,25},{25,1},{2,10},{10... | collective-permute-start | bytes 73736 | tf_op jit(solution)/shard_map/ppermute | solution.py:618
  6.4 10.5 %collective-permute-start.63 = (bf16[32,384]{1,0:T(8,128)(2,1)S(1)}, bf16[32,384]{1,0:T(8,128)(2,1)S(1)}, u32[]{:S(2)}, u32[]{:S(2)}) collective-permute-start(bf16[32,384]{1,0:T(8,128)(2,1)S(1)} %get-tuple-element.544), channel_id=1, source_target_pairs={{0,16},{8,24},{16,0},{24,8},{1,17},{9,25},{17,1},{25,9},{2,18},{10... | collective-permute-start | bytes 73736 | tf_op jit(solution)/shard_map/ppermute | solution.py:618
  8.7 8.2 %collective-permute-start.64 = (bf16[32,384]{1,0:T(8,128)(2,1)S(1)}, bf16[32,384]{1,0:T(8,128)(2,1)S(1)}, u32[]{:S(2)}, u32[]{:S(2)}) collective-permute-start(bf16[32,384]{1,0:T(8,128)(2,1)S(1)} %get-tuple-element.544), channel_id=1, source_target_pairs={{0,24},{8,0},{16,8},{24,16},{1,25},{9,1},{17,9},{25,17},{2,26},{10... | collective-permute-start | bytes 73736 | tf_op jit(solution)/shard_map/ppermute | solution.py:618
  10.1 6.8 %copy-start.4 = (s32[8]{0:T(128)S(1)}, s32[8]{0:T(128)}, u32[]{:S(2)}) copy-start(s32[8]{0:T(128)} %param.25) | copy-start | bytes 100
  10.1 6.8 %copy-start.5 = (bf16[384,768]{1,0:T(8,128)(2,1)S(1)}, bf16[384,768]{1,0:T(8,128)(2,1)}, u32[]{:S(2)}) copy-start(bf16[384,768]{1,0:T(8,128)(2,1)} %param.28) | copy-start | bytes 1769476
  17.0 7.4 %collective-permute-start.7 = (bf16[2,96,384]{2,1,0:T(8,128)(2,1)S(1)}, bf16[2,96,384]{2,1,0:T(8,128)(2,1)S(1)}, u32[]{:S(2)}, u32[]{:S(2)}) collective-permute-start(bf16[2,96,384]{2,1,0:T(8,128)(2,1)S(1)} %slice.54), channel_id=1, source_target_pairs={{0,4},{4,0},{1,5},{5,1},{2,6},{6,2},{3,7},{7,3},{8,12},{12,8},{9,1... | collective-permute-start | bytes 442376 | tf_op jit(solution)/shard_map/cond/branch_1_fun/ppermute | solution.py:624
  19.2 5.2 %collective-permute-start.6 = (f32[32,384]{1,0:T(8,128)S(1)}, f32[32,384]{1,0:T(8,128)S(1)}, u32[]{:S(2)}, u32[]{:S(2)}) collective-permute-start(f32[32,384]{1,0:T(8,128)S(1)} %get-tuple-element.306.refs_0_), channel_id=1, source_target_pairs={{0,4},{4,0},{1,5},{5,1},{2,6},{6,2},{3,7},{7,3},{8,12},{12,8},{9,1... | collective-permute-start | bytes 147464 | tf_op jit(solution)/shard_map/cond/branch_1_fun/ppermute | solution.py:618
  20.8 13.9 %collective-permute-start.12 = (bf16[2,160,384]{2,1,0:T(8,128)(2,1)S(1)}, bf16[2,160,384]{2,1,0:T(8,128)(2,1)S(1)}, u32[]{:S(2)}, u32[]{:S(2)}) collective-permute-start(bf16[2,160,384]{2,1,0:T(8,128)(2,1)S(1)} %slice.56), channel_id=1, source_target_pairs={{0,4},{4,0},{1,5},{5,1},{2,6},{6,2},{3,7},{7,3},{8,12},{12,8},{9,1... | collective-permute-start | bytes 737288 | tf_op jit(solution)/shard_map/cond/branch_1_fun/ppermute | solution.py:624
  21.4 15.3 %collective-permute-start.11 = (bf16[2,128,384]{2,1,0:T(8,128)(2,1)S(1)}, bf16[2,128,384]{2,1,0:T(8,128)(2,1)S(1)}, u32[]{:S(2)}, u32[]{:S(2)}) collective-permute-start(bf16[2,128,384]{2,1,0:T(8,128)(2,1)S(1)} %slice.55), channel_id=1, source_target_pairs={{0,4},{4,0},{1,5},{5,1},{2,6},{6,2},{3,7},{7,3},{8,12},{12,8},{9,1... | collective-permute-start | bytes 589832 | tf_op jit(solution)/shard_map/cond/branch_1_fun/ppermute | solution.py:624
  24.8 6.3 %collective-permute-start.10 = (f32[8,768]{1,0:T(8,128)S(1)}, f32[8,768]{1,0:T(8,128)S(1)}, u32[]{:S(2)}, u32[]{:S(2)}) collective-permute-start(f32[8,768]{1,0:T(8,128)S(1)} %get-tuple-element.309.refs_0_), channel_id=1, source_target_pairs={{0,3},{1,0},{2,1},{3,2},{4,7},{5,4},{6,5},{7,6},{8,11},{9,8},{10,9... | collective-permute-start | bytes 73736 | tf_op jit(solution)/shard_map/cond/branch_1_fun/ppermute | solution.py:618
  28.4 5.6 %collective-permute-start.8 = (f32[8,768]{1,0:T(8,128)S(1)}, f32[8,768]{1,0:T(8,128)S(1)}, u32[]{:S(2)}, u32[]{:S(2)}) collective-permute-start(f32[8,768]{1,0:T(8,128)S(1)} %get-tuple-element.309.refs_0_), channel_id=1, source_target_pairs={{0,1},{1,2},{2,3},{3,0},{4,5},{5,6},{6,7},{7,4},{8,9},{9,10},{10,1... | collective-permute-start | bytes 73736 | tf_op jit(solution)/shard_map/cond/branch_1_fun/ppermute | solution.py:618
  28.4 5.6 %collective-permute-start.9 = (f32[8,768]{1,0:T(8,128)S(1)}, f32[8,768]{1,0:T(8,128)S(1)}, u32[]{:S(2)}, u32[]{:S(2)}) collective-permute-start(f32[8,768]{1,0:T(8,128)S(1)} %get-tuple-element.309.refs_0_), channel_id=1, source_target_pairs={{0,2},{1,3},{2,0},{3,1},{4,6},{5,7},{6,4},{7,5},{8,10},{9,11},{10,... | collective-permute-start | bytes 73736 | tf_op jit(solution)/shard_map/cond/branch_1_fun/ppermute | solution.py:618

commit v3 on v2

--- a/solution.py
+++ b/solution.py
@@ -208,6 +208,7 @@
     req, pos, width = keys.shape
     half = pos // 2
     hbm = pl.BlockSpec(memory_space=pl.ANY)
+    smem = pl.BlockSpec(memory_space=pltpu.SMEM)
     vmem = pl.BlockSpec(memory_space=pltpu.VMEM)
     return pl.pallas_call(
         functools.partial(first_kernel, n_seq),
@@ -215,11 +216,11 @@
             pltpu.VMEM((2, FIRST * SLOTS, width), jnp.bfloat16),
             pltpu.VMEM((fresh.shape[0] + req, width), jnp.bfloat16),
             jax.ShapeDtypeStruct((1,), jnp.int32),
+            pltpu.SMEM(lengths.shape, jnp.int32),
         ),
         in_specs=[hbm] * 7,
-        out_specs=(vmem, vmem, pl.BlockSpec(memory_space=pltpu.SMEM)),
+        out_specs=(vmem, vmem, smem, smem),
         scratch_shapes=[
-            pltpu.SMEM(lengths.shape, jnp.int32),
             pltpu.VMEM((req, half), jnp.int32),
             pltpu.VMEM((req, half), jnp.float32),
             pltpu.VMEM(fresh.shape, fresh.dtype),
@@ -236,10 +237,10 @@
 
 
 def own_kernel(
-    n_seq, len_ref, keep, weight, gates, keys, values, early, *rest
+    n_seq, lengths, keep, weight, gates, keys, values, early, *rest
 ):
     out_k, out_v, chunk, rows, log_ref, level_ref, total_ref = rest[:7]
-    lengths, raw, late, forget, zeros, sem_s, sem_l, sem_r, sem_o, sem_z = rest[7:]
+    raw, late, forget, zeros, sem_l, sem_r, sem_o, sem_z = rest[7:]
     own, sent = half_of("seq", n_seq)
     seq = lax.axis_index("seq")
     heads, req, pos = gates.shape
@@ -248,7 +249,6 @@
     most = half // BLOCK
     first = FIRST // most
     pad = forget.shape[1] // req
-    small = fetch([(len_ref, lengths)], sem_s)
     both = ((0, keys), (1, values))
     channels = keys.shape[2]
 
@@ -278,8 +278,6 @@
         (2, chunk.shape[1] - FIRST * SLOTS, chunk.shape[2]), chunk.dtype
     )
     upto, block, after = block_masks(half)
-    for copy in small:
-        copy.wait()
     ahead, alive, _ = offsets(lengths, seq * pos + sent * half, most)
 
     forget[...] = jnp.zeros_like(forget)
@@ -372,15 +370,13 @@
             pltpu.VMEM((2, req * pad, slots), jnp.float32),
             pltpu.VMEM((req * pad, LANES), jnp.float32),
         ),
-        in_specs=[vmem] * 4 + [hbm] * 2 + [vmem],
+        in_specs=[pl.BlockSpec(memory_space=pltpu.SMEM)] + [vmem] * 3 + [hbm] * 2 + [vmem],
         out_specs=(hbm, hbm, vmem, vmem, vmem, vmem, vmem),
         scratch_shapes=[
-            pltpu.SMEM(lengths.shape, jnp.int32),
             pltpu.VMEM((req, half, 2 * width), jnp.bfloat16),
             pltpu.VMEM((late, half, 2 * width), jnp.bfloat16),
             pltpu.VMEM((pos // LANES, req * pad, LANES), jnp.float32),
             pltpu.VMEM((req, slots, width), jnp.bfloat16),
-            pltpu.SemaphoreType.DMA((1,)),
             pltpu.SemaphoreType.DMA((2 * late,)),
             pltpu.SemaphoreType.DMA((2 * req,)),
             pltpu.SemaphoreType.DMA((2 * req,)),
@@ -389,20 +385,20 @@
         compiler_params=pltpu.CompilerParams(vmem_limit_bytes=VMEM_LIMIT),
         cost_estimate=LIGHT,
         name="compact_own",
-    )(*near(lengths, keep, weight, forget), *far(keys, values), *near(early))
+    )(lengths, *near(keep, weight, forget), *far(keys, values), *near(early))
 
 
 def attend_kernel(n_seq, n_grp, heads, *refs):
-    len_hbm, route_hbm, own_rows, late, level, total = refs[:6]
+    lengths, route_hbm, own_rows, late, level, total = refs[:6]
     tokens, rest = refs[6 : 6 + n_grp], refs[6 + n_grp :]
-    stats_ref, picked_ref, lengths, route, scores, sem_s = rest
+    stats_ref, picked_ref, route, scores, sem_s = rest
     _, sent = half_of("seq", n_seq)
     kinds, width = picked_ref.shape
     req = kinds // 4
     size = width // heads
     slots = own_rows.shape[2]
     pad = total.shape[0] // req
-    small = fetch([(len_hbm, lengths), (route_hbm, route)], sem_s)
+    small = fetch([(route_hbm, route)], sem_s)
     for copy in small:
         copy.wait()
     start = lax.axis_index("seq") * (4 * slots) + sent * (2 * slots)
@@ -456,18 +452,17 @@
     return pl.pallas_call(
         functools.partial(attend_kernel, n_seq, n_grp, heads),
         out_shape=(small, small),
-        in_specs=[vmem] * (6 + n_grp),
+        in_specs=[pl.BlockSpec(memory_space=pltpu.SMEM)] + [vmem] * (5 + n_grp),
         out_specs=(vmem, vmem),
         scratch_shapes=[
-            pltpu.SMEM(lengths.shape, jnp.int32),
             pltpu.SMEM(route.shape, jnp.int32),
             pltpu.VMEM((total.shape[0], 2 * slots), jnp.float32),
-            pltpu.SemaphoreType.DMA((2,)),
+            pltpu.SemaphoreType.DMA((1,)),
         ],
         compiler_params=pltpu.CompilerParams(vmem_limit_bytes=VMEM_LIMIT),
         cost_estimate=LIGHT,
         name="attend",
-    )(*near(lengths, route, own_rows, late, level, total), *near(*tokens))
+    )(lengths, *near(route, own_rows, late, level, total), *near(*tokens))
 
 
 def merge_kernel(count, relative, size, *refs):
@@ -548,13 +543,12 @@
     )(*parts, later, logs, placed)
 
 
-def place_kernel(n_seq, first, count, *refs):
+def place_kernel(n_seq, first, count, marked, *refs):
     parts, refs = refs[:count], refs[count:]
-    len_ref, _, _, out_k, out_v, placed_ref, lengths, sem_s, sem = refs
+    lengths, _, _, out_k, out_v, *placed_ref, sem = refs
     _, sent = half_of("seq", n_seq)
-    (load,) = fetch([(len_ref, lengths)], sem_s)
-    placed_ref[...] = jnp.zeros_like(placed_ref)
-    load.wait()
+    if marked:
+        placed_ref[0][...] = jnp.zeros_like(placed_ref[0])
     req, rows, _ = out_k.shape
     slots = rows // 2
     most = slots // SLOTS
@@ -590,26 +584,25 @@
             begin += held
 
 
-def place_part(n_seq, first, parts, lengths, out_k, out_v):
+def place_part(n_seq, first, parts, lengths, out_k, out_v, marked=False):
     hbm = pl.BlockSpec(memory_space=pl.ANY)
+    smem = pl.BlockSpec(memory_space=pltpu.SMEM)
     vmem = pl.BlockSpec(memory_space=pltpu.VMEM)
     shape = pltpu.HBM(out_k.shape, out_k.dtype)
     count = len(parts)
     return pl.pallas_call(
-        functools.partial(place_kernel, n_seq, first, count),
-        out_shape=(shape, shape, pltpu.VMEM((8, LANES), jnp.float32)),
-        in_specs=[vmem] * (count + 1) + [hbm, hbm],
-        out_specs=(hbm, hbm, vmem),
+        functools.partial(place_kernel, n_seq, first, count, marked),
+        out_shape=(shape, shape) + (pltpu.VMEM((8, LANES), jnp.float32),) * marked,
+        in_specs=[vmem] * count + [smem, hbm, hbm],
+        out_specs=(hbm, hbm) + (vmem,) * marked,
         scratch_shapes=[
-            pltpu.SMEM(lengths.shape, jnp.int32),
-            pltpu.SemaphoreType.DMA((1,)),
             pltpu.SemaphoreType.DMA((count, 2, lengths.shape[0])),
         ],
         input_output_aliases={count + 1: 0, count + 2: 1},
         compiler_params=pltpu.CompilerParams(vmem_limit_bytes=VMEM_LIMIT),
         cost_estimate=LIGHT,
         name="place_received",
-    )(*near(*parts, lengths), *far(out_k, out_v))
+    )(*near(*parts), lengths, *far(out_k, out_v))
 
 
 def others(value, axis):
@@ -631,7 +624,7 @@
     heads = log_forget.shape[1]
     size = width // heads
     n_seq, n_grp = lax.axis_size("seq"), lax.axis_size("grp")
-    early, packed, choice = first_part(
+    early, packed, choice, held_lengths = first_part(
         n_seq,
         lengths,
         keep,
@@ -646,7 +639,7 @@
     tokens = others(packed, "grp")
     out_k, out_v, late, own_rows, logs, level, total = own_part(
         n_seq,
-        lengths,
+        held_lengths,
         keep,
         merge_weight,
         log_forget.transpose(1, 0, 2),
@@ -669,18 +662,20 @@
             gathered = lax.all_gather(stats, "seq")
             all_stats = [gathered[i] for i in range(n_seq)]
         ends = [end, end + rows]
-        if rows > 2 * LAST * SLOTS:
+        if rows > 3 * LAST * SLOTS:
             ends.insert(1, end + rows - LAST * SLOTS)
         third = [exchange(late[:, low:high]) for low, high in zip(ends, ends[1:])]
         later, partial = merge_part(all_stats, n_seq == 2, picked, out_weight, second, size)
-        out_k, out_v, placed = place_part(n_seq, 0, (early, second), lengths, out_k, out_v)
+        out_k, out_v, placed = place_part(
+            n_seq, 0, (early, second), lengths, out_k, out_v, marked=True
+        )
         layer_out, decay = sum_part(others(partial, "head"), later, logs, placed, size)
         for low, part in zip(ends, third):
-            out_k, out_v, _ = place_part(n_seq, low // SLOTS, (part,), lengths, out_k, out_v)
+            out_k, out_v = place_part(n_seq, low // SLOTS, (part,), lengths, out_k, out_v)
         return decay, layer_out, out_k, out_v
 
     operands = (first_received, late, own_rows, logs, level, total, tokens)
-    operands += (out_weight, lengths, route, out_k, out_v)
+    operands += (out_weight, held_lengths, route, out_k, out_v)
     if n_seq == 2:
         branches = [
             functools.partial(finish, blocks * SLOTS) for blocks in SIZES + (rest // SLOTS,)

time: 38.2 us -> 37.4 us (0.979)
  the two profiles are of different devices: /device:TPU:0 before, /device:TPU:30 now
where the time goes in v3:
time: 37.4 us
  Pallas kernels  14.5 us (39%)
  waiting for transfers between devices  11.9 us (32%)
  starting transfers between devices  9.27 us (25%)
  between operations  1.52 us (4%)
    ppermute x4, waiting for transfers between devices, swap(): return lax.ppermute(value, 'seq', [(0, 1), (1, 0)]) if n_seq == 2 else value  6.39 us
    pallas_call x1, Pallas kernels, own_part(): pl.pallas_call(functools.partial(own_kernel, n_seq), out_shape=(whole, wh...  6.26 us
    ppermute x7, starting transfers between devices, others(): lax.ppermute(value, axis, [(i, (i + k) % count) for i in range(count)])  6.16 us
    ppermute x7, waiting for transfers between devices, others(): lax.ppermute(value, axis, [(i, (i + k) % count) for i in range(count)])  5.54 us
    ppermute x4, starting transfers between devices, swap(): return lax.ppermute(value, 'seq', [(0, 1), (1, 0)]) if n_seq == 2 else value  3.11 us
    pallas_call x3, Pallas kernels, place_part(): pl.pallas_call(functools.partial(place_kernel, n_seq, first, count, marke...  2.82 us
    pallas_call x1, Pallas kernels, first_part(): pl.pallas_call(functools.partial(first_kernel, n_seq), out_shape=(pltpu.V...  2.72 us
    pallas_call x1, Pallas kernels, attend_part(): pl.pallas_call(functools.partial(attend_kernel, n_seq, n_grp, heads), out...  1.62 us
  transfers between devices with their start and end apart: 11, of which 7 were waited for; matrix products, arithmetic and copies ran while one was open for 0% of the time, Pallas kernels for 29%

profile of v3, /device:TPU:30, one launch (start us, length us, event | category | flops | bytes accessed | tf_op | source)
XLA Modules:
  0.0 37.4 jit_solution(11897043718306344779)
XLA Ops:
  0.6 0.0 copy-start
  0.6 0.0 copy-start.1
  0.7 0.0 copy-start.2
  0.7 2.7 %compact_first_sent.1 = (bf16[2,256,384]{2,1,0:T(8,128)(2,1)S(1)}, bf16[32,384]{1,0:T(8,128)(2,1)S(1)}, s32[1]{0:T(128)}, s32[8]{0:T(128)S(4)}) custom-call(s32[8]{0:T(128)} %len_hbm.1, s32[8,512]{1,0:T(8,128)} %keep.1, f32[8,512]{1,0:T(8,128)} %weight.1, bf16[24,384]{1,0:T(8,128)(2,1)} %bitcast.5, bf16[8,6]{1,0:T(8,128)(2,1)} %gate_hbm.1, ...), custom_call_target="tpu_custom_call" | custom-call | flops 1 | bytes 1 | tf_op jit(solution)/shard_map/compact_first_sent/pallas_call | solution.py:213
  3.4 0.6 %collective-permute-start.63 = (bf16[2,256,384]{2,1,0:T(8,128)(2,1)S(1)}, bf16[2,256,384]{2,1,0:T(8,128)(2,1)S(1)}, u32[]{:S(2)}, u32[]{:S(2)}) collective-permute-start(bf16[2,256,384]{2,1,0:T(8,128)(2,1)S(1)} %get-tuple-element.537.early), channel_id=1, source_target_pairs={{0,4},{4,0},{1,5},{5,1},{2,6},{6,2},{3,7},{7,3},{8,12},{12,8},{9,1... | collective-permute-start | bytes 1179656 | tf_op jit(solution)/shard_map/ppermute | solution.py:617
  4.0 0.1 collective-permute-start.60
  4.0 0.5 %collective-permute-start.61 = (bf16[32,384]{1,0:T(8,128)(2,1)S(1)}, bf16[32,384]{1,0:T(8,128)(2,1)S(1)}, u32[]{:S(2)}, u32[]{:S(2)}) collective-permute-start(bf16[32,384]{1,0:T(8,128)(2,1)S(1)} %get-tuple-element.542), channel_id=1, source_target_pairs={{0,16},{8,24},{16,0},{24,8},{1,17},{9,25},{17,1},{25,9},{2,18},{10... | collective-permute-start | bytes 73736 | tf_op jit(solution)/shard_map/ppermute | solution.py:611
  4.5 1.4 %collective-permute-start.62 = (bf16[32,384]{1,0:T(8,128)(2,1)S(1)}, bf16[32,384]{1,0:T(8,128)(2,1)S(1)}, u32[]{:S(2)}, u32[]{:S(2)}) collective-permute-start(bf16[32,384]{1,0:T(8,128)(2,1)S(1)} %get-tuple-element.542), channel_id=1, source_target_pairs={{0,24},{8,0},{16,8},{24,16},{1,25},{9,1},{17,9},{25,17},{2,26},{10... | collective-permute-start | bytes 73736 | tf_op jit(solution)/shard_map/ppermute | solution.py:611
  6.0 0.0 copy-done
  6.0 0.0 copy-done.1
  6.0 0.0 copy-done.2
  6.0 0.0 copy-start.3
  6.0 0.0 copy-start.4
  6.0 6.3 %compact_own.1 = (bf16[8,256,384]{2,1,0:T(8,128)(2,1)}, bf16[8,256,384]{2,1,0:T(8,128)(2,1)}, bf16[2,1024,384]{2,1,0:T(8,128)(2,1)S(1)}, bf16[2,8,128,384]{3,2,1...) custom-call(s32[8]{0:T(128)S(4)} %get-tuple-element.536.lengths, ...), custom_call_target="tpu_custom_call" | custom-call | flops 1 | bytes 1 | tf_op jit(solution)/shard_map/compact_own/pallas_call | solution.py:362
  12.9 0.0 collective-permute-done.60
  12.9 0.0 collective-permute-done.61
  12.9 0.0 collective-permute-done.62
  12.9 2.1 %collective-permute-done.63 = bf16[2,256,384]{2,1,0:T(8,128)(2,1)S(1)} collective-permute-done((bf16[2,256,384]{2,1,0:T(8,128)(2,1)S(1)}, bf16[2,256,384]{2,1,0:T(8,128)(2,1)S(1)}, u32[]{:S(2)}, u32[]{:S(2)}) %collective-permute-start.63) | collective-permute-done | bytes 393248 | tf_op jit(solution)/shard_map/ppermute | solution.py:617
  15.0 0.0 copy-done.3
  15.0 0.0 copy-done.4
  15.0 22.2 %conditional.1 = (f32[6,8,256]{2,1,0:T(8,128)}, bf16[8,768]{1,0:T(8,128)(2,1)}, bf16[8,256,384]{2,1,0:T(8,128)(2,1)}, bf16[8,256,384]{2,1,0:T(8,128)(2,1)}) conditional(s32[]{:T(128)} %bitcast.1, (s32[8]{0:T(128)S(4)}, s32[8]{0:T(128)S(1)}, bf16[2,8,128,384]{3,2,1,0:T(8,128)(2,1)S(1)}, ...), branch_computations={%region_0.0_spmd, %region_1.0_spmd, %region_2.0_spmd, %region_3.0_... | conditional | flops 68719476736 | bytes 7569726 | solution.py:683
  15.0 0.4 collective-permute-start.40
  15.4 1.6 %attend.15 = (f32[32,384]{1,0:T(8,128)S(1)}, f32[32,384]{1,0:T(8,128)S(1)}) custom-call(s32[8]{0:T(128)S(4)} %get-tuple-element.432.refs_0_.refs_2_.refs_1_, s32[8]{0:T(128)S(1)} %get-tuple-element.433.refs_1_, bf16[2,8,128,384]{3,2,1,0:T(8,128)(2,1)S(1)} %get-tuple-element.434.refs_2_, bf16[2,1024,384]{2,1,0:T(8,128)(2,1)S(1)} %get-tuple-element.435.refs_3_, ...), custom_call_target="tpu_custom_call" | custom-call | flops 1 | bytes 1 | tf_op jit(solution)/shard_map/cond/branch_6_fun/attend/pallas_call | solution.py:452
  17.0 1.8 %collective-permute-start.39 = (f32[32,384]{1,0:T(8,128)S(1)}, f32[32,384]{1,0:T(8,128)S(1)}, u32[]{:S(2)}, u32[]{:S(2)}) collective-permute-start(f32[32,384]{1,0:T(8,128)S(1)} %get-tuple-element.442.refs_0_), channel_id=1, source_target_pairs={{0,4},{4,0},{1,5},{5,1},{2,6},{6,2},{3,7},{7,3},{8,12},{12,8},{9,1... | collective-permute-start | bytes 147464 | tf_op jit(solution)/shard_map/cond/branch_6_fun/ppermute | solution.py:611
  18.8 0.1 slice.65
  18.9 0.3 collective-permute-start.45
  19.3 1.8 %collective-permute-start.44 = (bf16[2,128,384]{2,1,0:T(8,128)(2,1)S(1)}, bf16[2,128,384]{2,1,0:T(8,128)(2,1)S(1)}, u32[]{:S(2)}, u32[]{:S(2)}) collective-permute-start(bf16[2,128,384]{2,1,0:T(8,128)(2,1)S(1)} %slice.64), channel_id=1, source_target_pairs={{0,4},{4,0},{1,5},{5,1},{2,6},{6,2},{3,7},{7,3},{8,12},{12,8},{9,1... | collective-permute-start | bytes 589832 | tf_op jit(solution)/shard_map/cond/branch_6_fun/ppermute | solution.py:617
  21.1 1.4 %collective-permute-done.39.refs_1_ = f32[32,384]{1,0:T(8,128)S(1)} collective-permute-done((f32[32,384]{1,0:T(8,128)S(1)}, f32[32,384]{1,0:T(8,128)S(1)}, u32[]{:S(2)}, u32[]{:S(2)}) %collective-permute-start.39) | collective-permute-done | bytes 49184 | tf_op jit(solution)/shard_map/cond/branch_6_fun/ppermute | solution.py:611
  22.5 0.0 collective-permute-done.40.refs_4_.refs_1_
  22.5 0.3 merge_and_project.15
  22.8 0.2 collective-permute-start.41
  23.1 1.7 %collective-permute-start.42 = (f32[8,768]{1,0:T(8,128)S(1)}, f32[8,768]{1,0:T(8,128)S(1)}, u32[]{:S(2)}, u32[]{:S(2)}) collective-permute-start(f32[8,768]{1,0:T(8,128)S(1)} %get-tuple-element.445.refs_0_), channel_id=1, source_target_pairs={{0,2},{1,3},{2,0},{3,1},{4,6},{5,7},{6,4},{7,5},{8,10},{9,11},{10,... | collective-permute-start | bytes 73736 | tf_op jit(solution)/shard_map/cond/branch_6_fun/ppermute | solution.py:611
  24.8 0.4 %collective-permute-start.43 = (f32[8,768]{1,0:T(8,128)S(1)}, f32[8,768]{1,0:T(8,128)S(1)}, u32[]{:S(2)}, u32[]{:S(2)}) collective-permute-start(f32[8,768]{1,0:T(8,128)S(1)} %get-tuple-element.445.refs_0_), channel_id=1, source_target_pairs={{0,3},{1,0},{2,1},{3,2},{4,7},{5,4},{6,5},{7,6},{8,11},{9,8},{10,9... | collective-permute-start | bytes 73736 | tf_op jit(solution)/shard_map/cond/branch_6_fun/ppermute | solution.py:611
  25.2 1.1 %place_received.39 = (bf16[8,256,384]{2,1,0:T(8,128)(2,1)}, bf16[8,256,384]{2,1,0:T(8,128)(2,1)}, f32[8,128]{1,0:T(8,128)S(1)}) custom-call(bf16[2,256,384]{2,1,0:T(8,128)(2,1)S(1)} %get-tuple-element.448.refs_0_, bf16[2,96,384]{2,1,0:T(8,128)(2,1)S(1)} %collective-permute-done.40.refs_4_.refs_1_, ...), custom_call_target="tpu_custom_call", output_to_operand_aliasing={{0}: (3, {}), {1}: (4, {})} | custom-call | flops 1 | bytes 1 | tf_op jit(solution)/shard_map/cond/branch_6_fun/place_received/pallas_call | solution.py:593
  26.3 0.4 %collective-permute-done.41.refs_1_ = f32[8,768]{1,0:T(8,128)S(1)} collective-permute-done((f32[8,768]{1,0:T(8,128)S(1)}, f32[8,768]{1,0:T(8,128)S(1)}, u32[]{:S(2)}, u32[]{:S(2)}) %collective-permute-start.41) | collective-permute-done | bytes 24608 | tf_op jit(solution)/shard_map/cond/branch_6_fun/ppermute | solution.py:611
  26.7 1.1 %collective-permute-done.42.refs_2_ = f32[8,768]{1,0:T(8,128)S(1)} collective-permute-done((f32[8,768]{1,0:T(8,128)S(1)}, f32[8,768]{1,0:T(8,128)S(1)}, u32[]{:S(2)}, u32[]{:S(2)}) %collective-permute-start.42) | collective-permute-done | bytes 24608 | tf_op jit(solution)/shard_map/cond/branch_6_fun/ppermute | solution.py:611
  27.8 2.6 %collective-permute-done.43.refs_3_ = f32[8,768]{1,0:T(8,128)S(1)} collective-permute-done((f32[8,768]{1,0:T(8,128)S(1)}, f32[8,768]{1,0:T(8,128)S(1)}, u32[]{:S(2)}, u32[]{:S(2)}) %collective-permute-start.43) | collective-permute-done | bytes 24608 | tf_op jit(solution)/shard_map/cond/branch_6_fun/ppermute | solution.py:611
  30.4 0.7 %sum_heads_and_decay.15 = (bf16[8,768]{1,0:T(8,128)(2,1)}, f32[6,8,256]{2,1,0:T(8,128)}) custom-call(f32[8,768]{1,0:T(8,128)S(1)} %get-tuple-element.445.refs_0_, f32[8,768]{1,0:T(8,128)S(1)} %collective-permute-done.41.refs_1_, f32[8,768]{1,0:T(8,128)S(1)} %collective-permute-done.42.refs_2_, f32[8,768]{1,0:T(8,128)S(1)} %collective-permute-done.43.refs_3_, ...), custom_call_target="tpu_custom_call" | custom-call | flops 1 | bytes 1 | tf_op jit(solution)/shard_map/cond/branch_6_fun/sum_heads_and_decay/pallas_call | solution.py:532
  31.1 3.2 %collective-permute-done.45.refs_0_ = bf16[2,416,384]{2,1,0:T(8,128)(2,1)S(1)} collective-permute-done((bf16[2,416,384]{2,1,0:T(8,128)(2,1)S(1)}, bf16[2,416,384]{2,1,0:T(8,128)(2,1)S(1)}, u32[]{:S(2)}, u32[]{:S(2)}) %collective-permute-start.45) | collective-permute-done | bytes 639008 | tf_op jit(solution)/shard_map/cond/branch_6_fun/ppermute | solution.py:617
  34.3 0.9 %place_received.40 = (bf16[8,256,384]{2,1,0:T(8,128)(2,1)}, bf16[8,256,384]{2,1,0:T(8,128)(2,1)}) custom-call(bf16[2,416,384]{2,1,0:T(8,128)(2,1)S(1)} %collective-permute-done.45.refs_0_, s32[8]{0:T(128)S(4)} %get-tuple-element.432.refs_0_.refs_2_.refs_1_, ...), custom_call_target="tpu_custom_call", output_to_operand_aliasing={{0}: (2, {}), {1}: (3, {})} | custom-call | flops 1 | bytes 1 | tf_op jit(solution)/shard_map/cond/branch_6_fun/place_received/pallas_call | solution.py:593
  35.2 1.1 %collective-permute-done.44.refs_0_ = bf16[2,128,384]{2,1,0:T(8,128)(2,1)S(1)} collective-permute-done((bf16[2,128,384]{2,1,0:T(8,128)(2,1)S(1)}, bf16[2,128,384]{2,1,0:T(8,128)(2,1)S(1)}, u32[]{:S(2)}, u32[]{:S(2)}) %collective-permute-start.44) | collective-permute-done | bytes 196640 | tf_op jit(solution)/shard_map/cond/branch_6_fun/ppermute | solution.py:617
  36.4 0.8 %place_received.41 = (bf16[8,256,384]{2,1,0:T(8,128)(2,1)}, bf16[8,256,384]{2,1,0:T(8,128)(2,1)}) custom-call(bf16[2,128,384]{2,1,0:T(8,128)(2,1)S(1)} %collective-permute-done.44.refs_0_, s32[8]{0:T(128)S(4)} %get-tuple-element.432.refs_0_.refs_2_.refs_1_, ...), custom_call_target="tpu_custom_call", output_to_operand_aliasing={{0}: (2, {}), {1}: (3, {})} | custom-call | flops 1 | bytes 1 | tf_op jit(solution)/shard_map/cond/branch_6_fun/place_received/pallas_call | solution.py:593
  (2 shorter events, 0.0 us)
Async XLA Ops:
  0.6 5.3 %copy-start = (f32[8,6,512]{2,0,1:T(8,128)S(1)}, f32[8,6,512]{2,0,1:T(8,128)}, u32[]{:S(2)}) copy-start(f32[8,6,512]{2,0,1:T(8,128)} %param.21) | copy-start | bytes 294916
  0.6 5.3 %copy-start.1 = (s32[8,512]{1,0:T(8,128)S(1)}, s32[8,512]{1,0:T(8,128)}, u32[]{:S(2)}) copy-start(s32[8,512]{1,0:T(8,128)} %keep.1) | copy-start | bytes 49156
  0.7 5.3 %copy-start.2 = (f32[8,512]{1,0:T(8,128)S(1)}, f32[8,512]{1,0:T(8,128)}, u32[]{:S(2)}) copy-start(f32[8,512]{1,0:T(8,128)} %weight.1) | copy-start | bytes 49156
  3.4 11.6 %collective-permute-start.63 = (bf16[2,256,384]{2,1,0:T(8,128)(2,1)S(1)}, bf16[2,256,384]{2,1,0:T(8,128)(2,1)S(1)}, u32[]{:S(2)}, u32[]{:S(2)}) collective-permute-start(bf16[2,256,384]{2,1,0:T(8,128)(2,1)S(1)} %get-tuple-element.537.early), channel_id=1, source_target_pairs={{0,4},{4,0},{1,5},{5,1},{2,6},{6,2},{3,7},{7,3},{8,12},{12,8},{9,1... | collective-permute-start | bytes 1179656 | tf_op jit(solution)/shard_map/ppermute | solution.py:617
  4.0 8.9 %collective-permute-start.60 = (bf16[32,384]{1,0:T(8,128)(2,1)S(1)}, bf16[32,384]{1,0:T(8,128)(2,1)S(1)}, u32[]{:S(2)}, u32[]{:S(2)}) collective-permute-start(bf16[32,384]{1,0:T(8,128)(2,1)S(1)} %get-tuple-element.542), channel_id=1, source_target_pairs={{0,8},{8,16},{16,24},{24,0},{1,9},{9,17},{17,25},{25,1},{2,10},{10... | collective-permute-start | bytes 73736 | tf_op jit(solution)/shard_map/ppermute | solution.py:611
  4.0 8.9 %collective-permute-start.61 = (bf16[32,384]{1,0:T(8,128)(2,1)S(1)}, bf16[32,384]{1,0:T(8,128)(2,1)S(1)}, u32[]{:S(2)}, u32[]{:S(2)}) collective-permute-start(bf16[32,384]{1,0:T(8,128)(2,1)S(1)} %get-tuple-element.542), channel_id=1, source_target_pairs={{0,16},{8,24},{16,0},{24,8},{1,17},{9,25},{17,1},{25,9},{2,18},{10... | collective-permute-start | bytes 73736 | tf_op jit(solution)/shard_map/ppermute | solution.py:611
  4.5 8.4 %collective-permute-start.62 = (bf16[32,384]{1,0:T(8,128)(2,1)S(1)}, bf16[32,384]{1,0:T(8,128)(2,1)S(1)}, u32[]{:S(2)}, u32[]{:S(2)}) collective-permute-start(bf16[32,384]{1,0:T(8,128)(2,1)S(1)} %get-tuple-element.542), channel_id=1, source_target_pairs={{0,24},{8,0},{16,8},{24,16},{1,25},{9,1},{17,9},{25,17},{2,26},{10... | collective-permute-start | bytes 73736 | tf_op jit(solution)/shard_map/ppermute | solution.py:611
  6.0 9.0 %copy-start.3 = (s32[8]{0:T(128)S(1)}, s32[8]{0:T(128)}, u32[]{:S(2)}) copy-start(s32[8]{0:T(128)} %param.25) | copy-start | bytes 100
  6.0 9.0 %copy-start.4 = (bf16[384,768]{1,0:T(8,128)(2,1)S(1)}, bf16[384,768]{1,0:T(8,128)(2,1)}, u32[]{:S(2)}) copy-start(bf16[384,768]{1,0:T(8,128)(2,1)} %param.28) | copy-start | bytes 1769476
  15.0 7.5 %collective-permute-start.40 = (bf16[2,96,384]{2,1,0:T(8,128)(2,1)S(1)}, bf16[2,96,384]{2,1,0:T(8,128)(2,1)S(1)}, u32[]{:S(2)}, u32[]{:S(2)}) collective-permute-start(bf16[2,96,384]{2,1,0:T(8,128)(2,1)S(1)} %slice.63), channel_id=1, source_target_pairs={{0,4},{4,0},{1,5},{5,1},{2,6},{6,2},{3,7},{7,3},{8,12},{12,8},{9,1... | collective-permute-start | bytes 442376 | tf_op jit(solution)/shard_map/cond/branch_6_fun/ppermute | solution.py:617
  17.0 5.5 %collective-permute-start.39 = (f32[32,384]{1,0:T(8,128)S(1)}, f32[32,384]{1,0:T(8,128)S(1)}, u32[]{:S(2)}, u32[]{:S(2)}) collective-permute-start(f32[32,384]{1,0:T(8,128)S(1)} %get-tuple-element.442.refs_0_), channel_id=1, source_target_pairs={{0,4},{4,0},{1,5},{5,1},{2,6},{6,2},{3,7},{7,3},{8,12},{12,8},{9,1... | collective-permute-start | bytes 147464 | tf_op jit(solution)/shard_map/cond/branch_6_fun/ppermute | solution.py:611
  18.9 15.4 %collective-permute-start.45 = (bf16[2,416,384]{2,1,0:T(8,128)(2,1)S(1)}, bf16[2,416,384]{2,1,0:T(8,128)(2,1)S(1)}, u32[]{:S(2)}, u32[]{:S(2)}) collective-permute-start(bf16[2,416,384]{2,1,0:T(8,128)(2,1)S(1)} %slice.65), channel_id=1, source_target_pairs={{0,4},{4,0},{1,5},{5,1},{2,6},{6,2},{3,7},{7,3},{8,12},{12,8},{9,1... | collective-permute-start | bytes 1916936 | tf_op jit(solution)/shard_map/cond/branch_6_fun/ppermute | solution.py:617
  19.3 17.1 %collective-permute-start.44 = (bf16[2,128,384]{2,1,0:T(8,128)(2,1)S(1)}, bf16[2,128,384]{2,1,0:T(8,128)(2,1)S(1)}, u32[]{:S(2)}, u32[]{:S(2)}) collective-permute-start(bf16[2,128,384]{2,1,0:T(8,128)(2,1)S(1)} %slice.64), channel_id=1, source_target_pairs={{0,4},{4,0},{1,5},{5,1},{2,6},{6,2},{3,7},{7,3},{8,12},{12,8},{9,1... | collective-permute-start | bytes 589832 | tf_op jit(solution)/shard_map/cond/branch_6_fun/ppermute | solution.py:617
  22.8 3.9 %collective-permute-start.41 = (f32[8,768]{1,0:T(8,128)S(1)}, f32[8,768]{1,0:T(8,128)S(1)}, u32[]{:S(2)}, u32[]{:S(2)}) collective-permute-start(f32[8,768]{1,0:T(8,128)S(1)} %get-tuple-element.445.refs_0_), channel_id=1, source_target_pairs={{0,1},{1,2},{2,3},{3,0},{4,5},{5,6},{6,7},{7,4},{8,9},{9,10},{10,1... | collective-permute-start | bytes 73736 | tf_op jit(solution)/shard_map/cond/branch_6_fun/ppermute | solution.py:611
  23.1 4.7 %collective-permute-start.42 = (f32[8,768]{1,0:T(8,128)S(1)}, f32[8,768]{1,0:T(8,128)S(1)}, u32[]{:S(2)}, u32[]{:S(2)}) collective-permute-start(f32[8,768]{1,0:T(8,128)S(1)} %get-tuple-element.445.refs_0_), channel_id=1, source_target_pairs={{0,2},{1,3},{2,0},{3,1},{4,6},{5,7},{6,4},{7,5},{8,10},{9,11},{10,... | collective-permute-start | bytes 73736 | tf_op jit(solution)/shard_map/cond/branch_6_fun/ppermute | solution.py:611
  24.8 5.6 %collective-permute-start.43 = (f32[8,768]{1,0:T(8,128)S(1)}, f32[8,768]{1,0:T(8,128)S(1)}, u32[]{:S(2)}, u32[]{:S(2)}) collective-permute-start(f32[8,768]{1,0:T(8,128)S(1)} %get-tuple-element.445.refs_0_), channel_id=1, source_target_pairs={{0,3},{1,0},{2,1},{3,2},{4,7},{5,4},{6,5},{7,6},{8,11},{9,8},{10,9... | collective-permute-start | bytes 73736 | tf_op jit(solution)/shard_map/cond/branch_6_fun/ppermute | solution.py:611
